TPU v7x, 512 devices: a whole 4x8x8 slice. The times are simulated.
512 devices in a mesh: grp: 16 (over y, core), pair: 32 (over x, z).
Axes of the slice: x: 4, y: 8, z: 8, core: 2. Of those that a mesh axis runs over, the one named last changes fastest.
Arguments:
- amplitudes: bfloat16 [2048, 10368], P('pair'), may hold values from -6 to 6
- integrals: bfloat16 [10368, 10368], P('pair', 'grp'), may hold values from -0.0625 to 0.0625
- hole_ints: bfloat16 [2048, 2048], replicated, may hold values from -0.125 to 0.125
- driver: bfloat16 [2048, 10368], P('pair', 'grp'), may hold values from -6 to 6
- e_occ: float32 [128], replicated, may hold values from -1.2 to -0.2
- e_virt: float32 [288], replicated, may hold values from 0.3 to 1.5
- occ_pairs: int32 [2, 2048], P(None, 'pair'), may hold values from 0 to 127
- virt_pairs: int32 [2, 10368], P(None, 'grp'), may hold values from 0 to 287
Outputs:
- amp_next: float32 [2048, 10368], P('pair')
All inputs are finite; a program needn't handle non-finite values.
Results may differ from a plain program's by a relative error of at most 0.0003.
Values may be sent and summed in bfloat16 or wider, within the bound.
A program may use at most 128 MiB of HBM per device.

v0:
```python
import jax
import jax.numpy as jnp
from jax import lax
from jax.sharding import PartitionSpec as P


def lookup(labels, energies):
    table = lax.broadcasted_iota(jnp.int32, labels.shape + energies.shape, labels.ndim)
    picked = jnp.where(labels[..., None] == table, energies, jnp.float32(0.0))
    return jnp.sum(picked, axis=-1)


def shards(amplitudes, integrals, hole_ints, driver, e_occ, e_virt, occ_pairs, virt_pairs):
    row_count = amplitudes.shape[0]
    col_count = integrals.shape[1]
    col_start = lax.axis_index("grp") * col_count
    own_cols = lax.dynamic_slice_in_dim(amplitudes, col_start, col_count, 1)
    row_start = lax.axis_index("pair") * row_count
    left = amplitudes
    ladder = jnp.dot(
        left,
        lax.all_gather(integrals, "pair", axis=0, tiled=True),
        preferred_element_type=jnp.float32,
    )
    my_holes = lax.dynamic_slice_in_dim(hole_ints, row_start, row_count, 0)
    left = my_holes
    ladder = ladder + jnp.dot(
        left,
        lax.all_gather(own_cols, "pair", axis=0, tiled=True),
        preferred_element_type=jnp.float32,
    )
    occ_energy = lookup(occ_pairs, e_occ)
    virt_energy = lookup(virt_pairs, e_virt)
    hole_energy = occ_energy[0] + occ_energy[1]
    pair_energy = virt_energy[0] + virt_energy[1]
    energy_gap = pair_energy[None, :] - hole_energy[:, None]
    update = (driver.astype(jnp.float32) + ladder) / energy_gap
    return lax.all_gather(update, "grp", axis=1, tiled=True)


def solution(mesh):
    placed = (
        P("pair", None),
        P("pair", "grp"),
        P(),
        P("pair", "grp"),
        P(),
        P(),
        P(None, "pair"),
        P(None, "grp"),
    )
    return jax.shard_map(
        shards, mesh=mesh, in_specs=placed, out_specs=P("pair", None), check_vma=False
    )
```

profile of v0, /device:TPU:1, one launch (start us, length us, event | category | flops | bytes accessed | tf_op | source)
XLA Modules:
  0.0 304.6 jit_solution(4692069028827881941)
XLA Ops:
  6.5 0.0 copy-start
  6.5 0.0 all-gather.8.cloned.1.call-start
  6.5 0.7 all-gather.8.cloned.1.call-update
  7.3 0.0 all-gather.6.cloned.1.call-start
  7.3 0.5 copy-done
  7.9 0.7 constant_dynamic-slice_fusion
  8.6 0.0 all-gather.6.cloned.1.call-update
  8.6 0.0 all-gather.10.cloned.1.call-start
  8.7 1.0 select_reduce_fusion
  9.7 0.9 select_reduce_fusion.1
  10.6 147.6 %all-gather.8.cloned.1.call-done = bf16[32,324,648]{1,2,0:T(8,128)(2,1)} async-done(((bf16[1,324,648]{1,2,0:T(8,128)(2,1)}), bf16[32,324,648]{1,2,0:T(8,128)(2,1)}) %all-gather.8.cloned.1.call-update) | async-done | bytes 13436944 | tf_op jit(solution)/shard_map/all_gather | solution.py:22
  158.2 25.6 %copy.13 = bf16[32,324,648]{1,0,2:T(8,128)(2,1)} copy(bf16[32,324,648]{1,2,0:T(8,128)(2,1)} %all-gather.8.cloned.1.call-done) | data formatting | bytes 26873856 | tf_op jit(solution)/shard_map/all_gather | solution.py:22
  183.9 30.0 %reshape.13 = bf16[10368,648]{0,1:T(8,128)(2,1)} reshape(bf16[32,324,648]{1,0,2:T(8,128)(2,1)} %copy.13) | data formatting | bytes 26873856
  213.8 0.0 copy-start.1
  213.8 8.9 %fusion.6 = f32[64,648]{1,0:T(8,128)S(1)} fusion(bf16[64,10368]{1,0:T(8,128)(2,1)S(1)} %copy-done, bf16[10368,648]{0,1:T(8,128)(2,1)} %reshape.13), kind=kOutput, calls=%fused_computation.14 | convolution fusion | flops 859963392 | bytes 14929920 | tf_op jit(solution)/shard_map/dot_general | solution.py:20
  222.7 17.6 %all-gather.6.cloned.1.call-done = bf16[2048,648]{1,0:T(8,128)(2,1)} async-done(((bf16[64,648]{1,0:T(8,128)(2,1)}), bf16[2048,648]{1,0:T(8,128)(2,1)}) %all-gather.6.cloned.1.call-update) | async-done | bytes 2654224 | tf_op jit(solution)/shard_map/all_gather | solution.py:29
  240.3 0.0 copy-done.1
  240.4 3.3 %fusion.2 = f32[1,648,64]{1,2,0:T(8,128)} fusion(f32[64,648]{1,0:T(8,128)S(1)} %fusion.6, bf16[2048,648]{1,0:T(8,128)(2,1)} %all-gather.6.cloned.1.call-done, bf16[2048,2048]{1,0:T(8,128)(2,1)} %param.10, s32[]{:T(128)S(6)} %select_n.14, bf16[64,648]{1,0:T(8,128)(2,1)S(1)} %copy-done.1, f32[64]{0:T(128)S(1)} %add_bitcast_fusion, f32[648]{0:T(1024)S(1)} %fusion.4), kind=kOutput, calls=%fused_computation.5 | convolution fusion | flops 170076672 | bytes 3825444 | tf_op jit(solution)/shard_map/dot_general | solution.py:27
  243.7 0.0 all-gather.10.cloned.1.call-update
  243.7 44.3 %all-gather.10.cloned.1.call-done = f32[16,648,64]{1,2,0:T(8,128)} async-done(((f32[1,648,64]{1,2,0:T(8,128)}), f32[16,648,64]{1,2,0:T(8,128)}) %all-gather.10.cloned.1.call-update) | async-done | bytes 2654224 | tf_op jit(solution)/shard_map/all_gather | solution.py:38
  288.0 5.4 %copy.14 = f32[16,648,64]{1,0,2:T(8,128)} copy(f32[16,648,64]{1,2,0:T(8,128)} %all-gather.10.cloned.1.call-done) | data formatting | bytes 5308416 | tf_op jit(solution)/shard_map/all_gather | solution.py:38
  293.4 4.6 %reshape.15 = f32[10368,64]{0,1:T(8,128)} reshape(f32[16,648,64]{1,0,2:T(8,128)} %copy.14) | data formatting | bytes 5308416
  (2 shorter events, 0.0 us)
Async XLA Ops:
  6.5 1.3 copy-start
  6.5 151.7 %all-gather.8.cloned.1.call-start = ((), (), s32[]{:S(2)}) async-start(), calls=%async_computation.1 | async-start | bytes 16422912 | tf_op jit(solution)/shard_map/all_gather | solution.py:22
  7.3 233.1 %all-gather.6.cloned.1.call-start = ((), (), s32[]{:S(2)}) async-start(), calls=%async_computation | async-start | bytes 3244032 | tf_op jit(solution)/shard_map/all_gather | solution.py:29
  8.6 279.4 %all-gather.10.cloned.1.call-start = ((), (), s32[]{:S(2)}) async-start(), calls=%async_computation.2 | async-start | bytes 3342336 | tf_op jit(solution)/shard_map/all_gather | solution.py:38
  213.8 26.5 %copy-start.1 = (bf16[64,648]{1,0:T(8,128)(2,1)S(1)}, bf16[64,648]{1,0:T(8,128)(2,1)}, u32[]{:S(2)}) copy-start(bf16[64,648]{1,0:T(8,128)(2,1)} %param.11) | copy-start | bytes 248836
Sparse Core Ops, SparseCore 0:
  10.5 147.6 all-gather.7
  161.4 78.9 all-gather.5
  243.8 44.1 all-gather.9
where the time goes:
time: 306 us; the launch traced here: 305 us
  waiting for transfers between devices  210 us (69%)
  local copies, waits for them, and re-layouts  66.9 us (22%)
  between operations  13.1 us (4%)
  matrix products  12.2 us (4%)
    all_gather x1, waiting for transfers between devices, shards(): lax.all_gather(integrals, 'pair', axis=0, tiled=True)  148 us
    all_gather x1, waiting for transfers between devices, shards(): return lax.all_gather(update, 'grp', axis=1, tiled=True)  44.3 us
    unnamed x6, local copies, waits for them, and re-layouts  35.1 us
    all_gather x1, local copies, waits for them, and re-layouts, shards(): lax.all_gather(integrals, 'pair', axis=0, tiled=True)  25.6 us
    all_gather x1, waiting for transfers between devices, shards(): lax.all_gather(own_cols, 'pair', axis=0, tiled=True)  17.6 us
    dot_general x1, matrix products, shards(): jnp.dot(left, lax.all_gather(integrals, 'pair', axis=0, tiled=True), pref...  8.93 us
  transfers between devices with their start and end apart: 3, of which 3 were waited for; matrix products, arithmetic and copies ran while one was open for 22% of the time, Pallas kernels for 0%

commit v1 on v0

v1 whole, which is shorter than its diff:
```python
import functools

import jax
import jax.numpy as jnp
from jax import lax
from jax.experimental import pallas as pl
from jax.experimental.pallas import tpu as pltpu
from jax.sharding import PartitionSpec as P

MESH = pl.DeviceIdType.MESH
NX, NY, NZ = 4, 8, 8
ROWS = 64
DEPTH = 324
COLS = 648
LANES = 384
FRAME = 768
TALL = 656
VP = 10368
CHUNKS = ((0, 256, 256, 256), (256, 256, 256, 256), (512, 136, 144, 256))
FAR = (4, 3, 5, 2, 6, 1, 7)


def ladder_kernel(
    amp, ints, holes, drv, eocc, evirt, opairs, vpairs, out,
    amp_in, ints_in, drv_in, hole_win, eocc_in, evirt_in, opairs_in, vpairs_in,
    vt, ra, ap, al, part, rs, fin, fr, gap,
    in_sem, x_send, x_recv, a_send, a_recv, ad_send, ad_recv,
    z_send, z_recv, y_send, y_recv, c_send, c_recv, o_sem,
):
    grp, pair = lax.axis_index("grp"), lax.axis_index("pair")
    y, core = grp // 2, lax.rem(grp, 2)
    x, z = pair // NZ, lax.rem(pair, NZ)

    def at_x(d):
        return (grp, lax.rem(x + d, NX) * NZ + z)

    def at_z(d):
        return (grp, x * NZ + lax.rem(z + d, NZ))

    def at_y(d):
        return (lax.rem(y + d, NY) * 2 + core, pair)

    sibling = (y * 2 + 1 - core, pair)

    barrier = pltpu.get_barrier_semaphore()
    peers = [at_x(d) for d in (1, 2, 3)] + [at_z(d) for d in FAR]
    peers += [at_y(d) for d in FAR] + [sibling]
    for peer in peers:
        pl.semaphore_signal(barrier, inc=1, device_id=peer, device_id_type=MESH)

    loads = [
        pltpu.make_async_copy(ints, ints_in, in_sem.at[0]),
        pltpu.make_async_copy(amp, amp_in, in_sem.at[1]),
        pltpu.make_async_copy(drv, drv_in, in_sem.at[2]),
        pltpu.make_async_copy(eocc, eocc_in, in_sem.at[3]),
        pltpu.make_async_copy(evirt, evirt_in, in_sem.at[4]),
        pltpu.make_async_copy(opairs, opairs_in, in_sem.at[5]),
        pltpu.make_async_copy(vpairs, vpairs_in, in_sem.at[6]),
    ]
    for k in range(NX):
        rows = pl.ds(pl.multiple_of(x * NZ * ROWS, NZ * ROWS), NZ * ROWS)
        cols = pl.ds(pl.multiple_of((k * NZ + z) // 2 * 128, 128), 128)
        loads.append(
            pltpu.make_async_copy(holes.at[rows, cols], hole_win.at[k], in_sem.at[7 + k])
        )
    for load in loads:
        load.start()

    half = pl.multiple_of(lax.rem(z, 2) * ROWS, ROWS)
    other = pl.multiple_of(ROWS - lax.rem(z, 2) * ROWS, ROWS)

    loads[0].wait()
    vt[x] = jnp.zeros((TALL, LANES), jnp.bfloat16)
    vt[x, 0:COLS, 0:DEPTH] = ints_in[...]

    loads[1].wait()
    start = pl.multiple_of(grp * (COLS // 128) * 128, 128)
    window = amp_in[:, pl.ds(start, FRAME)].astype(jnp.float32)
    window = pltpu.roll(window, lax.rem(FRAME - grp * (COLS % 128), FRAME), axis=1)
    for k in range(NX):
        ra[k, pl.ds(other, ROWS), :] = jnp.zeros((ROWS, FRAME), jnp.bfloat16)
    ra[x, pl.ds(half, ROWS), :] = window.astype(jnp.bfloat16)

    ap[...] = jnp.zeros(ap.shape, jnp.bfloat16)
    for k in range(NX):
        for t in range(NZ):
            first = (k * NZ + t) * DEPTH
            ap[t, k, :, 0:DEPTH] = amp_in[:, first : first + DEPTH]

    pl.semaphore_wait(barrier, len(peers))

    started = []

    def send(src, dst, send_sem, recv_sem, device):
        copy = pltpu.make_async_remote_copy(
            src_ref=src, dst_ref=dst, send_sem=send_sem, recv_sem=recv_sem,
            device_id=device, device_id_type=MESH,
        )
        copy.start()
        started.append(copy)
        return copy

    both = pl.ds(2 * core, 2)
    a_copies = [
        send(ap.at[lax.rem(z + d, NZ), both], al.at[z, both],
             a_send.at[d - 1], a_recv.at[d - 1], at_z(d))
        for d in FAR
    ]
    x_copies = []
    for c, (first, _, tall, wide) in enumerate(CHUNKS):
        copies = []
        for d in (2, 1, 3):
            rows = (x, pl.ds(first, tall))
            copies.append(send(vt.at[rows], vt.at[rows], x_send.at[c, d - 1, 0],
                               x_recv.at[c, d - 1, 0], at_x(d)))
            cells = (x, pl.ds(half, ROWS), pl.ds(first, wide))
            copies.append(send(ra.at[cells], ra.at[cells], x_send.at[c, d - 1, 1],
                               x_recv.at[c, d - 1, 1], at_x(d)))
        x_copies.append(copies)

    al[z] = ap[z]

    for load in loads[2:]:
        load.wait()
    orbital = lax.broadcasted_iota(jnp.int32, (128, 128), 0)
    diagonal = orbital == lax.broadcasted_iota(jnp.int32, (128, 128), 1)

    def column(row):
        spread = jnp.where(diagonal, jnp.broadcast_to(row, (128, 128)), 0.0)
        return jnp.sum(spread, axis=1, keepdims=True)

    occ = column(eocc_in[...])
    hole_row = jnp.zeros((1, ROWS), jnp.float32)
    for s in range(2):
        labels = jnp.broadcast_to(opairs_in[s : s + 1, :], (128, ROWS))
        table = lax.broadcasted_iota(jnp.int32, (128, ROWS), 0)
        picked = jnp.where(labels == table, jnp.broadcast_to(occ, (128, ROWS)), 0.0)
        hole_row = hole_row + jnp.sum(picked, axis=0, keepdims=True)
    square = lax.broadcasted_iota(jnp.int32, (ROWS, ROWS), 0)
    square = square == lax.broadcasted_iota(jnp.int32, (ROWS, ROWS), 1)
    hole_col = jnp.sum(
        jnp.where(square, jnp.broadcast_to(hole_row, (ROWS, ROWS)), 0.0),
        axis=1, keepdims=True,
    )
    pair_row = jnp.zeros((1, COLS), jnp.float32)
    for s in range(2):
        labels = jnp.broadcast_to(vpairs_in[s : s + 1, :], (128, COLS))
        table = lax.broadcasted_iota(jnp.int32, (128, COLS), 0)
        picked = jnp.zeros((128, COLS), jnp.float32)
        for b in range(3):
            virt = jnp.broadcast_to(column(evirt_in[:, 128 * b : 128 * b + 128]), (128, COLS))
            picked = jnp.where(labels == table + 128 * b, virt, picked)
        pair_row = pair_row + jnp.sum(picked, axis=0, keepdims=True)
    gap[...] = pair_row - hole_col

    ad_copies = []
    for copy, d in zip(a_copies, FAR):
        copy.wait_recv()
        slot = al.at[lax.rem(z + NZ - d, NZ), both]
        ad_copies.append(send(slot, slot, ad_send.at[d - 1], ad_recv.at[d - 1], sibling))
    for copy in ad_copies:
        copy.wait_recv()

    z_copies = [None] * len(CHUNKS)
    y_copies = [None] * len(CHUNKS)

    def multiply(c):
        first, _, tall, wide = CHUNKS[c]
        for copy in x_copies[c]:
            copy.wait_recv()
        total = jnp.zeros((NZ * ROWS, tall), jnp.float32)
        for k in range(NX):
            total = total + lax.dot_general(
                al[:, k].reshape(NZ * ROWS, LANES), vt[k, first : first + tall, :],
                (((1,), (1,)), ((), ())), preferred_element_type=jnp.float32,
            )
            total = total + jnp.dot(
                hole_win[k], ra[k, :, first : first + tall],
                preferred_element_type=jnp.float32,
            )
        part[c, :, :, 0:tall] = total.reshape(NZ, ROWS, tall)
        z_copies[c] = [
            send(part.at[c, lax.rem(z + d, NZ)], rs.at[c, d - 1],
                 z_send.at[c, d - 1], z_recv.at[c, d - 1], at_z(d))
            for d in FAR
        ]

    def update(c):
        first, count, _, wide = CHUNKS[c]
        total = part[c, z, :, 0:count]
        for copy, d in zip(z_copies[c], FAR):
            copy.wait_recv()
            total = total + rs[c, d - 1, :, 0:count]
        driver = drv_in[:, first : first + count].astype(jnp.float32)
        fin[c, :, 0:count] = (driver + total) / gap[:, first : first + count]
        cols = pl.ds(first, wide)
        y_copies[c] = [
            send(fin.at[c], fr.at[d, :, cols], y_send.at[c, d - 1], y_recv.at[c, d - 1], at_y(d))
            for d in FAR
        ]
        c_copies.append(send(fin.at[c], out.at[grp, :, cols],
                             c_send.at[c, 0], c_recv.at[c, 0], sibling))
        copy = pltpu.make_async_copy(fin.at[c], out.at[grp, :, cols], o_sem.at[c, 0])
        copy.start()
        o_copies.append(copy)

    c_copies, o_copies = [], []

    def spread(c):
        first, _, _, wide = CHUNKS[c]
        cols = pl.ds(first, wide)
        for copy, d in zip(y_copies[c], FAR):
            copy.wait_recv()
            owner = lax.rem(y + NY - d, NY) * 2 + core
            c_copies.append(send(fr.at[d, :, cols], out.at[owner, :, cols],
                                 c_send.at[c, d], c_recv.at[c, d], sibling))
            copy = pltpu.make_async_copy(fr.at[d, :, cols], out.at[owner, :, cols], o_sem.at[c, d])
            copy.start()
            o_copies.append(copy)

    multiply(0)
    multiply(1)
    update(0)
    multiply(2)
    update(1)
    update(2)
    for c in range(len(CHUNKS)):
        spread(c)
    for copy in c_copies:
        copy.wait_recv()
    for copy in o_copies:
        copy.wait()
    for copy in started:
        copy.wait_send()


def place_kernel(blocks, out):
    for g in range(2 * NY):
        out[:, COLS * g : COLS * (g + 1)] = blocks[g, :, 0:COLS]


def shards(amplitudes, integrals, hole_ints, driver, e_occ, e_virt, occ_pairs, virt_pairs):
    chunks = len(CHUNKS)
    dma = pltpu.SemaphoreType.DMA
    virt = jnp.pad(e_virt, (0, 96)).reshape(1, 384)
    blocks = pl.pallas_call(
        ladder_kernel,
        out_shape=jax.ShapeDtypeStruct((2 * NY, ROWS, FRAME), jnp.float32),
        in_specs=[pl.BlockSpec(memory_space=pl.ANY)] * 8,
        out_specs=pl.BlockSpec(memory_space=pl.ANY),
        scratch_shapes=[
            pltpu.VMEM((ROWS, VP), jnp.bfloat16),
            pltpu.VMEM((COLS, DEPTH), jnp.bfloat16),
            pltpu.VMEM((ROWS, COLS), jnp.bfloat16),
            pltpu.VMEM((NX, NZ * ROWS, 128), jnp.bfloat16),
            pltpu.VMEM((1, 128), jnp.float32),
            pltpu.VMEM((1, 384), jnp.float32),
            pltpu.VMEM((2, ROWS), jnp.int32),
            pltpu.VMEM((2, COLS), jnp.int32),
            pltpu.VMEM((NX, TALL, LANES), jnp.bfloat16),
            pltpu.VMEM((NX, 2 * ROWS, FRAME), jnp.bfloat16),
            pltpu.VMEM((NZ, NX, ROWS, LANES), jnp.bfloat16),
            pltpu.VMEM((NZ, NX, ROWS, LANES), jnp.bfloat16),
            pltpu.VMEM((chunks, NZ, ROWS, 256), jnp.float32),
            pltpu.VMEM((chunks, NZ - 1, ROWS, 256), jnp.float32),
            pltpu.VMEM((chunks, ROWS, 256), jnp.float32),
            pltpu.VMEM((NY, ROWS, FRAME), jnp.float32),
            pltpu.VMEM((ROWS, COLS), jnp.float32),
            dma((11,)),
            dma((chunks, 3, 2)), dma((chunks, 3, 2)),
            dma((7,)), dma((7,)),
            dma((7,)), dma((7,)),
            dma((chunks, 7)), dma((chunks, 7)),
            dma((chunks, 7)), dma((chunks, 7)),
            dma((chunks, 8)), dma((chunks, 8)),
            dma((chunks, 8)),
        ],
        compiler_params=pltpu.CompilerParams(
            collective_id=0, has_side_effects=True, vmem_limit_bytes=40 * 2**20
        ),
        cost_estimate=pl.CostEstimate(
            flops=2 * NZ * ROWS * 4 * (DEPTH + ROWS) * COLS,
            bytes_accessed=8 * 2**20, transcendentals=0,
        ),
    )(
        amplitudes, integrals.T, hole_ints, driver, e_occ.reshape(1, 128), virt,
        occ_pairs, virt_pairs,
    )
    tall = 16
    return pl.pallas_call(
        place_kernel,
        grid=(ROWS // tall,),
        out_shape=jax.ShapeDtypeStruct((ROWS, VP), jnp.float32),
        in_specs=[pl.BlockSpec((2 * NY, tall, FRAME), lambda i: (0, i, 0))],
        out_specs=pl.BlockSpec((tall, VP), lambda i: (i, 0)),
        compiler_params=pltpu.CompilerParams(vmem_limit_bytes=32 * 2**20),
    )(blocks)


def solution(mesh):
    placed = (
        P("pair", None),
        P("pair", "grp"),
        P(),
        P("pair", "grp"),
        P(),
        P(),
        P(None, "pair"),
        P(None, "grp"),
    )
    return jax.shard_map(
        shards, mesh=mesh, in_specs=placed, out_specs=P("pair", None), check_vma=False
    )
```

time: 306 us -> 100 us (0.33)
  waiting for transfers between devices: 210 us -> 0 us
  Pallas kernels: 0 us -> 90.5 us
  local copies, waits for them, and re-layouts: 66.9 us -> 9.34 us
  between operations: 13.1 us -> 0.02 us
  matrix products: 12.2 us -> 0 us
    all_gather x3 -> x0, waiting for transfers between devices: 210 us -> none  [the longest x1 148 us: shards(): lax.all_gather(integrals, 'pair', axis=0, tiled=True)]
    pallas_call x0 -> x2, Pallas kernels: none -> 90.5 us  [the longest x1 87.9 us: shards(): pl.pallas_call(ladder_kernel, out_shape=jax.ShapeDtypeStruct((2 * NY, ROW...]
    all_gather x2 -> x0, local copies, waits for them, and re-layouts: 31 us -> none  [the longest x1 25.6 us: shards(): lax.all_gather(integrals, 'pair', axis=0, tiled=True)]
    unnamed x6 -> x14, local copies, waits for them, and re-layouts: 35.1 us -> 8.65 us
    dot_general x2 -> x0, matrix products: 12.2 us -> none  [the longest x1 8.93 us: shards(): jnp.dot(left, lax.all_gather(integrals, 'pair', axis=0, tiled=True), pref...]
  transfers between devices with their start and end apart: 3 -> 0, of which waited for: 3 -> 0; matrix products, arithmetic and copies ran while one was open for 22% -> 0% of each run, Pallas kernels for 0% -> 0%
where the time goes in v1:
time: 100 us; the launch traced here: 99.9 us
  Pallas kernels  90.5 us (90%)
  local copies, waits for them, and re-layouts  9.34 us (9%)
    pallas_call x1, Pallas kernels, shards(): pl.pallas_call(ladder_kernel, out_shape=jax.ShapeDtypeStruct((2 * NY, ROW...  87.9 us
    unnamed x14, local copies, waits for them, and re-layouts  8.65 us
    pallas_call x1, Pallas kernels, shards(): pl.pallas_call(place_kernel, grid=(ROWS // tall,), out_shape=jax.ShapeDty...  2.65 us

profile of v1, /device:TPU:1, one launch (start us, length us, event | category | flops | bytes accessed | tf_op | source)
XLA Modules:
  0.0 99.9 jit_solution(14745651081429107015)
XLA Ops:
  0.0 0.7 pad.4
  0.7 0.0 copy-start
  0.7 3.4 %copy-done = bf16[2048,2048]{1,0:T(8,128)(2,1)S(1)} copy-done((bf16[2048,2048]{1,0:T(8,128)(2,1)S(1)}, bf16[2048,2048]{1,0:T(8,128)(2,1)}, u32[]{:S(2)}) %copy-start) | copy-done | bytes 8388632
  4.1 0.0 copy-start.1
  4.1 1.3 %copy-done.1 = bf16[64,10368]{1,0:T(8,128)(2,1)S(1)} copy-done((bf16[64,10368]{1,0:T(8,128)(2,1)S(1)}, bf16[64,10368]{1,0:T(8,128)(2,1)}, u32[]{:S(2)}) %copy-start.1) | copy-done | bytes 1327128
  5.4 0.0 copy-start.2
  5.4 1.0 %copy-done.2 = bf16[324,648]{0,1:T(8,128)(2,1)S(1)} copy-done((bf16[324,648]{0,1:T(8,128)(2,1)S(1)}, bf16[324,648]{0,1:T(8,128)(2,1)}, u32[]{:S(2)}) %copy-start.2) | copy-done | bytes 419928
  6.4 0.0 copy-start.3
  6.4 0.9 copy-done.3
  7.3 0.0 copy-start.4
  7.3 0.7 copy-done.4
  8.0 0.0 copy-start.5
  8.0 0.7 copy-done.5
  8.7 0.0 copy-start.6
  8.7 0.7 copy-done.6
  9.3 87.9 %shard_map.82.blocks = f32[16,64,768]{2,1,0:T(8,128)S(1)} custom-call(bf16[64,10368]{1,0:T(8,128)(2,1)S(1)} %copy-done.1, bf16[648,324]{1,0:T(8,128)(2,1)S(1)} %bitcast.2, bf16[2048,2048]{1,0:T(8,128)(2,1)S(1)} %copy-done, bf16[64,648]{1,0:T(8,128)(2,1)S(1)} %copy-done.3, f32[1,128]{1,0:T(1,128)S(1)} %bitcast.3, f32[1,384]{1,0:T(1,128)S(1)} %reshape.7.evirt, ...), custom_call_target="tpu_custom_call" | custom-call | flops 1029832704 | bytes 8388608 | tf_op jit(solution)/shard_map/pallas_call | solution.py:246
  97.2 2.6 %shard_map.83 = f32[64,10368]{1,0:T(8,128)} custom-call(f32[16,64,768]{2,1,0:T(8,128)S(1)} %shard_map.82.blocks), custom_call_target="tpu_custom_call" | custom-call | tf_op jit(solution)/shard_map/pallas_call | solution.py:290
  (1 shorter events, 0.0 us)
Async XLA Ops:
  0.7 3.4 %copy-start = (bf16[2048,2048]{1,0:T(8,128)(2,1)S(1)}, bf16[2048,2048]{1,0:T(8,128)(2,1)}, u32[]{:S(2)}) copy-start(bf16[2048,2048]{1,0:T(8,128)(2,1)} %holes.1) | copy-start | bytes 25165828
  4.1 1.3 %copy-start.1 = (bf16[64,10368]{1,0:T(8,128)(2,1)S(1)}, bf16[64,10368]{1,0:T(8,128)(2,1)}, u32[]{:S(2)}) copy-start(bf16[64,10368]{1,0:T(8,128)(2,1)} %amp.1) | copy-start | bytes 3981316
  5.4 1.0 %copy-start.2 = (bf16[324,648]{0,1:T(8,128)(2,1)S(1)}, bf16[324,648]{0,1:T(8,128)(2,1)}, u32[]{:S(2)}) copy-start(bf16[324,648]{0,1:T(8,128)(2,1)} %param.9) | copy-start | bytes 1259716
  6.4 0.9 copy-start.3
  7.3 0.7 copy-start.4
  8.0 0.7 copy-start.5
  8.7 0.7 copy-start.6

commit v2 on v1

v2 whole, which is shorter than its diff:
```python
import jax
import jax.numpy as jnp
from jax import lax
from jax.experimental import pallas as pl
from jax.experimental.pallas import tpu as pltpu
from jax.sharding import PartitionSpec as P

MESH = pl.DeviceIdType.MESH
NX, NY, NZ = 4, 8, 8
ROWS = 64
SET = NZ * ROWS
DEPTH = 324
COLS = 648
LANES = 384
FRAME = 768
TALL = 656
VP = 10368
WIDE = 256
LAST = 2 * WIDE
REST = COLS - LAST - 128
PACKED = ROWS + REST
FAR = (4, 3, 5, 2, 6, 1, 7)


def ladder_kernel(
    amp, ints, holes, drv, eocc, evirt, opairs, vpairs, out, out_last,
    amp_in, ints_in, drv_in, hole_win, eocc_in, evirt_in, opairs_in, vpairs_in,
    vt, ra, ap, al, part, part_last, via3, via4, rs, rs_last,
    fin, fin_last, fr, fr_last, gap, gap_last, drv_last,
    in_sem, x_send, x_recv, a_send, a_recv, ay_send, ay_recv, ad_send, ad_recv,
    z_send, z_recv, zl_send, zl_recv, y_send, y_recv, yl_send, yl_recv,
    c_send, c_recv, cl_send, cl_recv, o_sem, ol_sem,
):
    grp, pair = lax.axis_index("grp"), lax.axis_index("pair")
    y, core = grp // 2, lax.rem(grp, 2)
    x, z = pair // NZ, lax.rem(pair, NZ)

    def at_x(d):
        return (grp, lax.rem(x + d, NX) * NZ + z)

    def at_z(d):
        return (grp, x * NZ + lax.rem(z + d, NZ))

    def at_y(d):
        return (lax.rem(y + d, NY) * 2 + core, pair)

    sibling = (y * 2 + 1 - core, pair)

    barrier = pltpu.get_barrier_semaphore()
    peers = [at_x(d) for d in (1, 2, 3)] + [at_z(d) for d in FAR]
    peers += [at_y(d) for d in FAR] + [sibling]
    for peer in peers:
        pl.semaphore_signal(barrier, inc=1, device_id=peer, device_id_type=MESH)

    loads = [
        pltpu.make_async_copy(ints, ints_in, in_sem.at[0]),
        pltpu.make_async_copy(amp, amp_in, in_sem.at[1]),
        pltpu.make_async_copy(drv, drv_in, in_sem.at[2]),
        pltpu.make_async_copy(eocc, eocc_in, in_sem.at[3]),
        pltpu.make_async_copy(evirt, evirt_in, in_sem.at[4]),
        pltpu.make_async_copy(opairs, opairs_in, in_sem.at[5]),
        pltpu.make_async_copy(vpairs, vpairs_in, in_sem.at[6]),
    ]
    for k in range(NX):
        rows = pl.ds(pl.multiple_of(x * SET, SET), SET)
        cols = pl.ds(pl.multiple_of((k * NZ + z) // 2 * 128, 128), 128)
        loads.append(
            pltpu.make_async_copy(holes.at[rows, cols], hole_win.at[k], in_sem.at[7 + k])
        )
    for load in loads:
        load.start()

    half = pl.multiple_of(lax.rem(z, 2) * ROWS, ROWS)
    other = pl.multiple_of(ROWS - lax.rem(z, 2) * ROWS, ROWS)
    started = []

    def send(src, dst, send_sem, recv_sem, device):
        copy = pltpu.make_async_remote_copy(
            src_ref=src, dst_ref=dst, send_sem=send_sem, recv_sem=recv_sem,
            device_id=device, device_id_type=MESH,
        )
        copy.start()
        started.append(copy)
        return copy

    loads[0].wait()
    vt[x, COLS:TALL, :] = jnp.zeros((TALL - COLS, LANES), jnp.bfloat16)
    vt[x, 0:COLS, 256:LANES] = jnp.zeros((COLS, LANES - 256), jnp.bfloat16)
    vt[x, 0:COLS, 0:DEPTH] = ints_in[...]

    loads[1].wait()
    start = pl.multiple_of(grp * (COLS // 128) * 128, 128)
    window = amp_in[:, pl.ds(start, FRAME)].astype(jnp.float32)
    window = pltpu.roll(window, lax.rem(FRAME - grp * (COLS % 128), FRAME), axis=1)
    for k in range(NX):
        ra[k, pl.ds(other, ROWS), :] = jnp.zeros((ROWS, FRAME), jnp.bfloat16)
    ra[x, pl.ds(half, ROWS), :] = window.astype(jnp.bfloat16)

    for k in range(NX):
        for t in range(NZ):
            first = (k * NZ + t) * DEPTH
            ap[t, k, :, 256:LANES] = jnp.zeros((ROWS, LANES - 256), jnp.bfloat16)
            ap[t, k, :, 0:DEPTH] = amp_in[:, first : first + DEPTH]

    pl.semaphore_wait(barrier, len(peers))

    both = pl.ds(2 * core, 2)
    unit = y // 2
    unit_rows = pl.ds(pl.multiple_of(lax.rem(y, 2) * 32 + core * 16, 16), 16)
    far_copies = [
        send(ap.at[lax.rem(z + d, NZ), unit, unit_rows], al.at[NZ - d, unit, unit_rows],
             a_send.at[d - 1], a_recv.at[d - 1], at_z(d))
        for d in (4, 3, 5)
    ]

    def x_parts(c, which, part_of=None):
        first, tall, wide = c * WIDE, WIDE, WIDE
        if c == 2:
            tall = TALL - LAST
        if part_of is not None:
            first, tall, wide = first + 128 * part_of, 128, 128
        return vt.at[which, pl.ds(first, tall)], ra.at[which, pl.ds(half, ROWS), pl.ds(first, wide)]

    def x_sends(c, which, d, slot, part_of=None):
        return [
            send(ref, ref, x_send.at[c, slot, i], x_recv.at[c, slot, i], at_x(d))
            for i, ref in enumerate(x_parts(c, which, part_of))
        ]

    x_copies = [[], [], []]

    def x_first(c):
        x_copies[c] = [x_sends(c, x, 1, 0), x_sends(c, x, 3, 1)]

    def x_second(c):
        for copies in x_copies[c]:
            for copy in copies:
                copy.wait_recv()
        x_copies[c] = [
            x_sends(c, lax.rem(x + 3, NX), 1, 2, 0),
            x_sends(c, lax.rem(x + 1, NX), 3, 3, 1),
        ]

    x_first(0)
    near_copies = [
        send(ap.at[lax.rem(z + d, NZ), both], al.at[NZ - d, both],
             a_send.at[d - 1], a_recv.at[d - 1], at_z(d))
        for d in (2, 6, 1, 7)
    ]
    x_first(1)
    x_copies[2] = [x_sends(2, x, d, d - 1) for d in (2, 1, 3)]

    al[0] = ap[z]

    for load in loads[2:]:
        load.wait()
    orbital = lax.broadcasted_iota(jnp.int32, (128, 128), 0)
    diagonal = orbital == lax.broadcasted_iota(jnp.int32, (128, 128), 1)

    def column(row):
        spread = jnp.where(diagonal, jnp.broadcast_to(row, (128, 128)), 0.0)
        return jnp.sum(spread, axis=1, keepdims=True)

    occ = column(eocc_in[...])
    hole_row = jnp.zeros((1, ROWS), jnp.float32)
    for s in range(2):
        labels = jnp.broadcast_to(opairs_in[s : s + 1, :], (128, ROWS))
        table = lax.broadcasted_iota(jnp.int32, (128, ROWS), 0)
        picked = jnp.where(labels == table, jnp.broadcast_to(occ, (128, ROWS)), 0.0)
        hole_row = hole_row + jnp.sum(picked, axis=0, keepdims=True)
    square = lax.broadcasted_iota(jnp.int32, (ROWS, ROWS), 0)
    square = square == lax.broadcasted_iota(jnp.int32, (ROWS, ROWS), 1)
    hole_col = jnp.sum(
        jnp.where(square, jnp.broadcast_to(hole_row, (ROWS, ROWS)), 0.0),
        axis=1, keepdims=True,
    )
    padded = jnp.concatenate([evirt_in[...], jnp.zeros((1, 96), jnp.float32)], axis=1)
    virts = [column(padded[:, 128 * b : 128 * b + 128]) for b in range(3)]
    pair_row = jnp.zeros((1, COLS), jnp.float32)
    for s in range(2):
        labels = jnp.broadcast_to(vpairs_in[s : s + 1, :], (128, COLS))
        table = lax.broadcasted_iota(jnp.int32, (128, COLS), 0)
        picked = jnp.zeros((128, COLS), jnp.float32)
        for b in range(3):
            virt = jnp.broadcast_to(virts[b], (128, COLS))
            picked = jnp.where(labels == table + 128 * b, virt, picked)
        pair_row = pair_row + jnp.sum(picked, axis=0, keepdims=True)
    gap[...] = pair_row - hole_col

    def turned(block):
        tile = jnp.concatenate([block, jnp.zeros((ROWS, 128 - REST), jnp.float32)], axis=1)
        tile = jnp.concatenate([tile, jnp.zeros((128 - ROWS, 128), jnp.float32)], axis=0)
        return jnp.transpose(tile)[0:REST, 0:ROWS]

    gap_last[...] = jnp.ones(gap_last.shape, jnp.float32)
    gap_last[0:ROWS, :] = gap[:, LAST : LAST + 128]
    gap_last[ROWS:PACKED, 0:ROWS] = turned(gap[:, COLS - REST : COLS])
    drv_last[...] = jnp.zeros(drv_last.shape, jnp.float32)
    drv_last[0:ROWS, :] = drv_in[:, LAST : LAST + 128].astype(jnp.float32)
    drv_last[ROWS:PACKED, 0:ROWS] = turned(drv_in[:, COLS - REST : COLS].astype(jnp.float32))

    ad_copies = []

    def share(ref, slot):
        ad_copies.append(send(ref, ref, ad_send.at[slot], ad_recv.at[slot], sibling))

    far = pl.ds(3, 3)
    for copy in far_copies:
        copy.wait_recv()
    own = al.at[far, unit, unit_rows]
    ay_copies = [
        send(own, own, ay_send.at[d - 1], ay_recv.at[d - 1], at_y(d)) for d in FAR
    ]
    share(own, 0)
    x_second(0)
    for slot, (copy, d) in enumerate(zip(near_copies, (2, 6, 1, 7))):
        copy.wait_recv()
        share(al.at[NZ - d, both], 8 + slot)
    x_second(1)
    for copy, d in zip(ay_copies, FAR):
        copy.wait_recv()
        there = lax.rem(y + NY - d, NY)
        rows = pl.ds(pl.multiple_of(lax.rem(there, 2) * 32 + core * 16, 16), 16)
        share(al.at[far, there // 2, rows], d)
    for copy in ad_copies:
        copy.wait_recv()

    def product(c, first, tall, wide):
        for copies in x_copies[c]:
            for copy in copies:
                copy.wait_recv()
        total = jnp.zeros((SET, wide), jnp.float32)
        for k in range(NX):
            total = total + lax.dot_general(
                al[:, k].reshape(SET, LANES), vt[k, first : first + tall, :],
                (((1,), (1,)), ((), ())), preferred_element_type=jnp.float32,
            )
            lines = [
                hole_win[k, pl.ds(pl.multiple_of(lax.rem(z + r, NZ) * ROWS, ROWS), ROWS), :]
                for r in range(NZ)
            ]
            total = total + jnp.dot(
                jnp.concatenate(lines, axis=0), ra[k, :, first : first + wide],
                preferred_element_type=jnp.float32,
            )
        return total

    z_copies, y_copies = [None, None], [None, None]
    c_copies, o_copies = [], []

    def multiply(c):
        part[c] = product(c, c * WIDE, WIDE, WIDE).reshape(NZ, ROWS, WIDE)
        z_copies[c] = [
            send(part.at[c, 4, :, pl.ds(0, 128)], via4.at[c, 0], z_send.at[c, 0], z_recv.at[c, 0], at_z(2)),
            send(part.at[c, 4, :, pl.ds(128, 128)], via4.at[c, 1], z_send.at[c, 1], z_recv.at[c, 1], at_z(6)),
            send(part.at[c, 3], via3.at[c, 0], z_send.at[c, 2], z_recv.at[c, 2], at_z(1)),
            send(part.at[c, 5], via3.at[c, 1], z_send.at[c, 3], z_recv.at[c, 3], at_z(7)),
            send(part.at[c, 1], rs.at[c, 0], z_send.at[c, 4], z_recv.at[c, 4], at_z(1)),
            send(part.at[c, 7], rs.at[c, 1], z_send.at[c, 5], z_recv.at[c, 5], at_z(7)),
        ]

    def relay(c):
        for copy in z_copies[c][:4]:
            copy.wait_recv()
        part[c, 2] = part[c, 2] + via3[c, 0]
        part[c, 2, :, 0:128] = part[c, 2, :, 0:128] + via4[c, 0]
        part[c, 6] = part[c, 6] + via3[c, 1]
        part[c, 6, :, 128:256] = part[c, 6, :, 128:256] + via4[c, 1]
        z_copies[c] = z_copies[c][4:] + [
            send(part.at[c, 2], rs.at[c, 2], z_send.at[c, 6], z_recv.at[c, 6], at_z(2)),
            send(part.at[c, 6], rs.at[c, 3], z_send.at[c, 7], z_recv.at[c, 7], at_z(6)),
        ]

    def update(c):
        first = c * WIDE
        for copy in z_copies[c]:
            copy.wait_recv()
        total = part[c, 0] + ((rs[c, 0] + rs[c, 1]) + (rs[c, 2] + rs[c, 3]))
        driver = drv_in[:, first : first + WIDE].astype(jnp.float32)
        fin[c] = (driver + total) / gap[:, first : first + WIDE]
        cols = pl.ds(first, WIDE)
        y_copies[c] = [
            send(fin.at[c], fr.at[d, :, cols], y_send.at[c, i], y_recv.at[c, i], at_y(d))
            for i, d in enumerate((2, 6, 1, 7))
        ]
        keep(fin.at[c], 0, c)

    def y_relay(c):
        for copy in y_copies[c][:2]:
            copy.wait_recv()
        first = c * WIDE
        cols = pl.ds(first, WIDE)
        left, right = pl.ds(first, 128), pl.ds(first + 128, 128)
        moves = (
            (fr.at[2, :, left], fr.at[4, :, left], 2),
            (fr.at[6, :, right], fr.at[4, :, right], 6),
            (fr.at[2, :, cols], fr.at[3, :, cols], 1),
            (fr.at[6, :, cols], fr.at[5, :, cols], 7),
        )
        y_copies[c] += [
            send(src, dst, y_send.at[c, 4 + i], y_recv.at[c, 4 + i], at_y(d))
            for i, (src, dst, d) in enumerate(moves)
        ]

    def keep(ref, d, c):
        owner = lax.rem(y + NY - d, NY) * 2 + core
        dst = out.at[owner, :, pl.ds(c * WIDE, WIDE)] if c < 2 else out_last.at[owner]
        sems = (c_send.at[c, d], c_recv.at[c, d], o_sem.at[c, d])
        if c == 2:
            sems = (cl_send.at[d], cl_recv.at[d], ol_sem.at[d])
        c_copies.append(send(ref, dst, sems[0], sems[1], sibling))
        copy = pltpu.make_async_copy(ref, dst, sems[2])
        copy.start()
        o_copies.append(copy)

    def spread(c):
        cols = pl.ds(c * WIDE, WIDE)
        first, second = y_copies[c][:4], y_copies[c][4:]
        for copy, d in zip(first[2:], (1, 7)):
            copy.wait_recv()
            keep(fr.at[d, :, cols], d, c)
        for d in (2, 6):
            keep(fr.at[d, :, cols], d, c)
        for copy, d in zip(second[2:], (3, 5)):
            copy.wait_recv()
            keep(fr.at[d, :, cols], d, c)
        for copy in second[:2]:
            copy.wait_recv()
        keep(fr.at[4, :, cols], 4, c)

    def multiply_last():
        total = product(2, LAST, TALL - LAST, TALL - LAST)
        part_last[:, 0:ROWS, :] = total[:, 0:128].reshape(NZ, ROWS, 128)
        rest = jnp.concatenate(
            [total[:, 128:144], jnp.zeros((SET, 112), jnp.float32)], axis=1
        )
        for b in range(SET // 128):
            tile = jnp.transpose(rest[128 * b : 128 * b + 128])[0:REST]
            part_last[2 * b, ROWS:PACKED, 0:ROWS] = tile[:, 0:ROWS]
            part_last[2 * b + 1, ROWS:PACKED, 0:ROWS] = tile[:, ROWS : 2 * ROWS]
        return [
            send(part_last.at[d], rs_last.at[d - 1], zl_send.at[d - 1], zl_recv.at[d - 1], at_z(d))
            for d in FAR
        ]

    def update_last(copies):
        total = part_last[0]
        for copy, d in zip(copies, FAR):
            copy.wait_recv()
            total = total + rs_last[d - 1]
        fin_last[...] = (drv_last[...] + total) / gap_last[...]
        copies = [
            send(fin_last, fr_last.at[d], yl_send.at[d - 1], yl_recv.at[d - 1], at_y(d))
            for d in FAR
        ]
        keep(fin_last, 0, 2)
        return copies

    def spread_last(copies):
        for copy, d in zip(copies, FAR):
            copy.wait_recv()
            keep(fr_last.at[d], d, 2)

    part_last[:, ROWS:PACKED, :] = jnp.zeros((NZ, REST, 128), jnp.float32)
    multiply(0)
    multiply(1)
    relay(0)
    relay(1)
    update(0)
    last = multiply_last()
    update(1)
    y_relay(0)
    last = update_last(last)
    y_relay(1)
    spread(0)
    spread(1)
    spread_last(last)
    for copy in c_copies:
        copy.wait_recv()
    for copy in o_copies:
        copy.wait()
    for copy in started:
        copy.wait_send()


def place_kernel(blocks, last, out, rest):
    tall = out.shape[0]
    step = pl.program_id(0)

    @pl.when(step == 0)
    def _():
        for g in range(2 * NY):
            tile = jnp.concatenate(
                [last[g, ROWS:PACKED, :], jnp.zeros((128 - REST, 128), jnp.float32)], axis=0
            )
            rest[g] = jnp.transpose(tile)[0:ROWS, :]

    rows = pl.ds(pl.multiple_of(step * tall, tall), tall)
    for g in range(2 * NY):
        first = COLS * g
        out[:, first : first + LAST] = blocks[g]
        out[:, first + LAST : first + LAST + 128] = last[g, rows, :]
        out[:, first + COLS - REST : first + COLS] = rest[g, rows, 0:REST]


def shards(amplitudes, integrals, hole_ints, driver, e_occ, e_virt, occ_pairs, virt_pairs):
    dma = pltpu.SemaphoreType.DMA
    bf16, f32 = jnp.bfloat16, jnp.float32
    blocks, last = pl.pallas_call(
        ladder_kernel,
        out_shape=[
            jax.ShapeDtypeStruct((2 * NY, ROWS, LAST), f32),
            jax.ShapeDtypeStruct((2 * NY, PACKED, 128), f32),
        ],
        in_specs=[pl.BlockSpec(memory_space=pl.ANY)] * 8,
        out_specs=[pl.BlockSpec(memory_space=pl.ANY)] * 2,
        scratch_shapes=[
            pltpu.VMEM((ROWS, VP), bf16),
            pltpu.VMEM((COLS, DEPTH), bf16),
            pltpu.VMEM((ROWS, COLS), bf16),
            pltpu.VMEM((NX, SET, 128), bf16),
            pltpu.VMEM((1, 128), f32),
            pltpu.VMEM((1, 288), f32),
            pltpu.VMEM((2, ROWS), jnp.int32),
            pltpu.VMEM((2, COLS), jnp.int32),
            pltpu.VMEM((NX, TALL, LANES), bf16),
            pltpu.VMEM((NX, 2 * ROWS, FRAME), bf16),
            pltpu.VMEM((NZ, NX, ROWS, LANES), bf16),
            pltpu.VMEM((NZ, NX, ROWS, LANES), bf16),
            pltpu.VMEM((2, NZ, ROWS, WIDE), f32),
            pltpu.VMEM((NZ, PACKED, 128), f32),
            pltpu.VMEM((2, 2, ROWS, WIDE), f32),
            pltpu.VMEM((2, 2, ROWS, 128), f32),
            pltpu.VMEM((2, 4, ROWS, WIDE), f32),
            pltpu.VMEM((NZ - 1, PACKED, 128), f32),
            pltpu.VMEM((2, ROWS, WIDE), f32),
            pltpu.VMEM((PACKED, 128), f32),
            pltpu.VMEM((NY, ROWS, LAST), f32),
            pltpu.VMEM((NY, PACKED, 128), f32),
            pltpu.VMEM((ROWS, COLS), f32),
            pltpu.VMEM((PACKED, 128), f32),
            pltpu.VMEM((PACKED, 128), f32),
            dma((11,)),
            dma((3, 4, 2)), dma((3, 4, 2)),
            dma((7,)), dma((7,)),
            dma((7,)), dma((7,)),
            dma((12,)), dma((12,)),
            dma((2, 8)), dma((2, 8)), dma((7,)), dma((7,)),
            dma((2, 8)), dma((2, 8)), dma((7,)), dma((7,)),
            dma((2, 8)), dma((2, 8)), dma((8,)), dma((8,)),
            dma((2, 8)), dma((8,)),
        ],
        compiler_params=pltpu.CompilerParams(
            collective_id=0, has_side_effects=True, vmem_limit_bytes=62 * 2**20
        ),
        cost_estimate=pl.CostEstimate(
            flops=2 * SET * 4 * (DEPTH + ROWS) * COLS,
            bytes_accessed=8 * 2**20, transcendentals=0,
        ),
    )(
        amplitudes, integrals.T, hole_ints, driver, e_occ.reshape(1, 128),
        e_virt.reshape(1, 288), occ_pairs, virt_pairs,
    )
    tall = 16
    return pl.pallas_call(
        place_kernel,
        grid=(ROWS // tall,),
        out_shape=jax.ShapeDtypeStruct((ROWS, VP), f32),
        in_specs=[
            pl.BlockSpec((2 * NY, tall, LAST), lambda i: (0, i, 0)),
            pl.BlockSpec((2 * NY, PACKED, 128), lambda i: (0, 0, 0)),
        ],
        out_specs=pl.BlockSpec((tall, VP), lambda i: (i, 0)),
        scratch_shapes=[pltpu.VMEM((2 * NY, ROWS, 128), f32)],
        compiler_params=pltpu.CompilerParams(vmem_limit_bytes=62 * 2**20),
    )(blocks, last)


def solution(mesh):
    placed = (
        P("pair", None),
        P("pair", "grp"),
        P(),
        P("pair", "grp"),
        P(),
        P(),
        P(None, "pair"),
        P(None, "grp"),
    )
    return jax.shard_map(
        shards, mesh=mesh, in_specs=placed, out_specs=P("pair", None), check_vma=False
    )
```

time: 100 us -> 82.1 us (0.82)
  Pallas kernels: 90.5 us -> 80.6 us
  local copies, waits for them, and re-layouts: 9.34 us -> 1.24 us
    pallas_call x1, Pallas kernels: 87.9 us -> 75.9 us  [shards(): pl.pallas_call(ladder_kernel, out_shape=[jax.ShapeDtypeStruct((2 * NY, RO...]
    unnamed x14 -> x0, local copies, waits for them, and re-layouts: 8.65 us -> none
    pallas_call x1, Pallas kernels: 2.65 us -> 4.73 us  [shards(): pl.pallas_call(place_kernel, grid=(ROWS // tall,), out_shape=jax.ShapeDty...]
    reshape x1, local copies, waits for them, and re-layouts: 0.01 us -> 1.24 us  [shards(): e_virt.reshape(1, 288)]
where the time goes in v2:
time: 82.1 us; the launch traced here: 81.9 us
  Pallas kernels  80.6 us (98%)
  local copies, waits for them, and re-layouts  1.24 us (2%)
    pallas_call x1, Pallas kernels, shards(): pl.pallas_call(ladder_kernel, out_shape=[jax.ShapeDtypeStruct((2 * NY, RO...  75.9 us
    pallas_call x1, Pallas kernels, shards(): pl.pallas_call(place_kernel, grid=(ROWS // tall,), out_shape=jax.ShapeDty...  4.73 us

profile of v2, /device:TPU:1, one launch (start us, length us, event | category | flops | bytes accessed | tf_op | source)
XLA Modules:
  0.0 81.9 jit_solution(6598675782290104256)
XLA Ops:
  0.0 1.2 %reshape.7.evirt = f32[1,288]{1,0:T(1,128)} reshape(f32[288]{0:T(512)} %param.13) | data formatting | bytes 2304 | tf_op jit(solution)/shard_map/reshape | solution.py:462
  1.2 75.9 %shard_map.82 = (f32[16,64,512]{2,1,0:T(8,128)}, f32[16,72,128]{2,1,0:T(8,128)}) custom-call(bf16[64,10368]{1,0:T(8,128)(2,1)} %amp.1, bf16[648,324]{1,0:T(8,128)(2,1)} %bitcast.2, bf16[2048,2048]{1,0:T(8,128)(2,1)} %holes.1, bf16[64,648]{1,0:T(8,128)(2,1)} %drv.1, f32[1,128]{1,0:T(1,128)} %bitcast.3, f32[1,288]{1,0:T(1,128)} %reshape.7.evirt, ...), custom_call_target="tpu_custom_call" | custom-call | flops 1029832704 | bytes 8388608 | tf_op jit(solution)/shard_map/pallas_call | solution.py:409
  77.1 4.7 %shard_map.83 = f32[64,10368]{1,0:T(8,128)} custom-call(f32[16,64,512]{2,1,0:T(8,128)} %get-tuple-element.7.blocks, f32[16,72,128]{2,1,0:T(8,128)} %get-tuple-element.8.last), custom_call_target="tpu_custom_call" | custom-call | tf_op jit(solution)/shard_map/pallas_call | solution.py:465

commit v3 on v2

v3 whole, which is shorter than its diff:
```python
import jax
import jax.numpy as jnp
from jax import lax
from jax.experimental import pallas as pl
from jax.experimental.pallas import tpu as pltpu
from jax.sharding import PartitionSpec as P

MESH = pl.DeviceIdType.MESH
NX, NY, NZ = 4, 8, 8
ROWS = 64
SET = NZ * ROWS
DEPTH = 324
COLS = 648
LANES = 384
FRAME = 768
DEEP = NX * LANES
TALL = 656
VP = 10368
WIDE = 256
LAST = 2 * WIDE
REST = COLS - LAST - 128
PACKED = ROWS + REST
TILED = 80
TOP = 32767.0
TINY = 1e-33
FAR = (4, 3, 5, 2, 6, 1, 7)


def ladder_kernel(
    amp, ints, holes, drv, eocc, evirt, opairs, vpairs, out, out_last, out_scale,
    amp_in, ints_in, drv_in, hole_win, eocc_in, evirt_in, opairs_in, vpairs_in,
    own_vt, vt, ra, ap, al, hole_rel, part, part_last, via3, via3_last, via4, via4_last, rs, rs_last,
    scale, fr, fr_last, fr_scale, gap, gap_last, drv_last,
    in_sem, x_send, x_recv, a_send, a_recv, ay_send, ay_recv, ad_send, ad_recv,
    z_send, z_recv, y_send, y_recv, c_send, c_recv, o_sem,
):
    grp, pair = lax.axis_index("grp"), lax.axis_index("pair")
    y, core = grp // 2, lax.rem(grp, 2)
    x, z = pair // NZ, lax.rem(pair, NZ)

    def at_x(d):
        return (grp, lax.rem(x + d, NX) * NZ + z)

    def at_z(d):
        return (grp, x * NZ + lax.rem(z + d, NZ))

    def at_y(d):
        return (lax.rem(y + d, NY) * 2 + core, pair)

    sibling = (y * 2 + 1 - core, pair)

    barrier = pltpu.get_barrier_semaphore()
    peers = [at_x(d) for d in (1, 2, 3)] + [at_z(d) for d in FAR]
    peers += [at_y(d) for d in FAR] + [sibling]
    for peer in peers:
        pl.semaphore_signal(barrier, inc=1, device_id=peer, device_id_type=MESH)

    loads = [
        pltpu.make_async_copy(ints, ints_in, in_sem.at[0]),
        pltpu.make_async_copy(amp, amp_in, in_sem.at[1]),
        pltpu.make_async_copy(drv, drv_in, in_sem.at[2]),
        pltpu.make_async_copy(eocc, eocc_in, in_sem.at[3]),
        pltpu.make_async_copy(evirt, evirt_in, in_sem.at[4]),
        pltpu.make_async_copy(opairs, opairs_in, in_sem.at[5]),
        pltpu.make_async_copy(vpairs, vpairs_in, in_sem.at[6]),
    ]
    for k in range(NX):
        rows = pl.ds(pl.multiple_of(x * SET, SET), SET)
        cols = pl.ds(pl.multiple_of((k * NZ + z) // 2 * 128, 128), 128)
        loads.append(
            pltpu.make_async_copy(
                holes.at[rows, cols], hole_win.at[:, pl.ds(128 * k, 128)], in_sem.at[7 + k]
            )
        )
    for load in loads:
        load.start()

    half = pl.multiple_of(lax.rem(z, 2) * ROWS, ROWS)
    other = pl.multiple_of(ROWS - lax.rem(z, 2) * ROWS, ROWS)
    started = []

    def send(src, dst, send_sem, recv_sem, device):
        copy = pltpu.make_async_remote_copy(
            src_ref=src, dst_ref=dst, send_sem=send_sem, recv_sem=recv_sem,
            device_id=device, device_id_type=MESH,
        )
        copy.start()
        started.append(copy)
        return copy

    loads[0].wait()
    own_vt[COLS:TALL, :] = jnp.zeros((TALL - COLS, LANES), jnp.bfloat16)
    own_vt[0:COLS, 256:LANES] = jnp.zeros((COLS, LANES - 256), jnp.bfloat16)
    own_vt[0:COLS, 0:DEPTH] = ints_in[...]

    loads[1].wait()
    start = pl.multiple_of(grp * (COLS // 128) * 128, 128)
    window = amp_in[:, pl.ds(start, FRAME)].astype(jnp.float32)
    window = pltpu.roll(window, lax.rem(FRAME - grp * (COLS % 128), FRAME), axis=1)
    for k in range(NX):
        ra[pl.ds(128 * k + other, ROWS), :] = jnp.zeros((ROWS, FRAME), jnp.bfloat16)
    ra[pl.ds(128 * x + half, ROWS), :] = window.astype(jnp.bfloat16)

    for k in range(NX):
        for t in range(NZ):
            first = (k * NZ + t) * DEPTH
            at = k * LANES
            ap[t, :, at + 256 : at + LANES] = jnp.zeros((ROWS, LANES - 256), jnp.bfloat16)
            ap[t, :, at : at + DEPTH] = amp_in[:, first : first + DEPTH]

    pl.semaphore_wait(barrier, len(peers))

    both = pl.ds(pl.multiple_of(core * 2 * LANES, 128), 2 * LANES)

    def unit_of(chip):
        rows = pl.ds(pl.multiple_of(lax.rem(chip, 2) * 32 + core * 16, 16), 16)
        return rows, pl.ds(pl.multiple_of(chip // 2 * LANES, 128), LANES)

    rows, lanes = unit_of(y)
    far_copies = [
        send(ap.at[lax.rem(z + d, NZ), rows, lanes], al.at[NZ - d, rows, lanes],
             a_send.at[d - 1], a_recv.at[d - 1], at_z(d))
        for d in (4, 3, 5)
    ]

    def x_sends(c, owner, d, slot, side=None):
        first, tall, wide = c * WIDE, (TALL - LAST if c == 2 else WIDE), WIDE
        if side is not None:
            first, tall, wide = first + 128 * side, 128, 128
        to = vt.at[pl.ds(first, tall), pl.ds(pl.multiple_of(owner * LANES, 128), LANES)]
        cells = ra.at[pl.ds(pl.multiple_of(128 * owner + half, ROWS), ROWS), pl.ds(first, wide)]
        return [
            send(own_vt.at[pl.ds(first, tall)] if owner is x else to, to,
                 x_send.at[c, slot, 0], x_recv.at[c, slot, 0], at_x(d)),
            send(cells, cells, x_send.at[c, slot, 1], x_recv.at[c, slot, 1], at_x(d)),
        ]

    x_copies = [[], [], []]

    def x_first(c):
        x_copies[c] = [x_sends(c, x, 1, 0), x_sends(c, x, 3, 1)]

    def x_second(c):
        for copies in x_copies[c]:
            for copy in copies:
                copy.wait_recv()
        x_copies[c] = [
            x_sends(c, lax.rem(x + 3, NX), 1, 2, 0),
            x_sends(c, lax.rem(x + 1, NX), 3, 3, 1),
        ]

    x_first(0)
    near_copies = [
        send(ap.at[lax.rem(z + d, NZ), :, both], al.at[NZ - d, :, both],
             a_send.at[d - 1], a_recv.at[d - 1], at_z(d))
        for d in (2, 6, 1, 7)
    ]
    x_first(1)

    vt[:, pl.ds(pl.multiple_of(x * LANES, 128), LANES)] = own_vt[...]
    al[0] = ap[z]

    for load in loads[2:]:
        load.wait()
    orbital = lax.broadcasted_iota(jnp.int32, (128, 128), 0)
    diagonal = orbital == lax.broadcasted_iota(jnp.int32, (128, 128), 1)

    def column(row):
        spread = jnp.where(diagonal, jnp.broadcast_to(row, (128, 128)), 0.0)
        return jnp.sum(spread, axis=1, keepdims=True)

    occ = column(eocc_in[...])
    hole_row = jnp.zeros((1, ROWS), jnp.float32)
    for s in range(2):
        labels = jnp.broadcast_to(opairs_in[s : s + 1, :], (128, ROWS))
        table = lax.broadcasted_iota(jnp.int32, (128, ROWS), 0)
        picked = jnp.where(labels == table, jnp.broadcast_to(occ, (128, ROWS)), 0.0)
        hole_row = hole_row + jnp.sum(picked, axis=0, keepdims=True)
    square = lax.broadcasted_iota(jnp.int32, (ROWS, ROWS), 0)
    square = square == lax.broadcasted_iota(jnp.int32, (ROWS, ROWS), 1)
    hole_col = jnp.sum(
        jnp.where(square, jnp.broadcast_to(hole_row, (ROWS, ROWS)), 0.0),
        axis=1, keepdims=True,
    )
    padded = jnp.concatenate([evirt_in[...].reshape(1, 288), jnp.zeros((1, 96), jnp.float32)], axis=1)
    virts = [column(padded[:, 128 * b : 128 * b + 128]) for b in range(3)]
    pair_row = jnp.zeros((1, COLS), jnp.float32)
    for s in range(2):
        labels = jnp.broadcast_to(vpairs_in[s : s + 1, :], (128, COLS))
        table = lax.broadcasted_iota(jnp.int32, (128, COLS), 0)
        picked = jnp.zeros((128, COLS), jnp.float32)
        for b in range(3):
            virt = jnp.broadcast_to(virts[b], (128, COLS))
            picked = jnp.where(labels == table + 128 * b, virt, picked)
        pair_row = pair_row + jnp.sum(picked, axis=0, keepdims=True)
    gap[...] = pair_row - hole_col

    def turned(block):
        tile = jnp.concatenate([block, jnp.zeros((ROWS, 128 - REST), jnp.float32)], axis=1)
        tile = jnp.concatenate([tile, jnp.zeros((128 - ROWS, 128), jnp.float32)], axis=0)
        return jnp.transpose(tile)[0:REST, 0:ROWS]

    gap_last[...] = jnp.ones(gap_last.shape, jnp.float32)
    gap_last[0:ROWS, :] = gap[:, LAST : LAST + 128]
    gap_last[ROWS:PACKED, 0:ROWS] = turned(gap[:, COLS - REST : COLS])
    drv_last[...] = jnp.zeros(drv_last.shape, jnp.float32)
    drv_last[0:ROWS, :] = drv_in[:, LAST : LAST + 128].astype(jnp.float32)
    drv_last[ROWS:PACKED, 0:ROWS] = turned(drv_in[:, COLS - REST : COLS].astype(jnp.float32))

    for r in range(NZ):
        lines = pl.ds(pl.multiple_of(lax.rem(z + r, NZ) * ROWS, ROWS), ROWS)
        hole_rel[r * ROWS : (r + 1) * ROWS, :] = hole_win[lines, :]

    ad_copies = []

    def share(ref, slot):
        ad_copies.append(send(ref, ref, ad_send.at[slot], ad_recv.at[slot], sibling))

    far = pl.ds(3, 3)
    for copy in far_copies:
        copy.wait_recv()
    own = al.at[far, rows, lanes]
    ay_copies = [
        send(own, own, ay_send.at[d - 1], ay_recv.at[d - 1], at_y(d)) for d in FAR
    ]
    share(own, 0)
    x_second(0)
    x_copies[2] = [x_sends(2, x, d, d - 1) for d in (2, 1, 3)]
    for slot, (copy, d) in enumerate(zip(near_copies, (2, 6, 1, 7))):
        copy.wait_recv()
        share(al.at[NZ - d, :, both], 8 + slot)
    x_second(1)
    for copy, d in zip(ay_copies, FAR):
        copy.wait_recv()
        rows, lanes = unit_of(lax.rem(y + NY - d, NY))
        share(al.at[far, rows, lanes], d)
    for copy in ad_copies:
        copy.wait_recv()

    def product(c):
        first, tall = c * WIDE, (TALL - LAST if c == 2 else WIDE)
        for copies in x_copies[c]:
            for copy in copies:
                copy.wait_recv()
        return lax.dot_general(
            al[...].reshape(SET, DEEP), vt[first : first + tall, :],
            (((1,), (1,)), ((), ())), preferred_element_type=jnp.float32,
        ) + jnp.dot(
            hole_rel[...], ra[:, first : first + tall], preferred_element_type=jnp.float32
        )

    z_copies, z_later, y_copies = [None] * 3, [None] * 3, [None] * 3
    c_copies, o_copies = [], []

    sums = (part.at[0], part.at[1], part_last)
    via_3 = (via3.at[0], via3.at[1], via3_last)
    via_4 = (via4.at[0], via4.at[1], via4_last)
    landed = (rs.at[0], rs.at[1], rs_last)

    def sides(c):
        if c < 2:
            return (slice(0, ROWS), slice(0, 128)), (slice(0, ROWS), slice(128, 256))
        return (slice(0, 40), slice(0, 128)), (slice(40, PACKED), slice(0, 128))

    def z_send_to(c, i, src, dst, d):
        return send(src, dst, z_send.at[c, i], z_recv.at[c, i], at_z(d))

    def z_first(c):
        a, b = sides(c)
        at_b = (slice(0, PACKED - 40), slice(0, 128)) if c == 2 else (slice(0, ROWS), slice(0, 128))
        z_copies[c] = [
            z_send_to(c, 0, sums[c].at[(4,) + a], via_4[c].at[0], 2),
            z_send_to(c, 1, sums[c].at[(4,) + b], via_4[c].at[(1,) + at_b], 6),
            z_send_to(c, 2, sums[c].at[3], via_3[c].at[0], 1),
            z_send_to(c, 3, sums[c].at[5], via_3[c].at[1], 7),
        ]

    def z_direct(c):
        z_later[c] = [
            z_send_to(c, 4, sums[c].at[1], landed[c].at[0], 1),
            z_send_to(c, 5, sums[c].at[7], landed[c].at[1], 7),
        ]

    def relay(c):
        for copy in z_copies[c]:
            copy.wait_recv()
        a, b = sides(c)
        at_b = (slice(0, PACKED - 40), slice(0, 128)) if c == 2 else (slice(0, ROWS), slice(0, 128))
        store = sums[c]
        store[2] = store[2] + via_3[c][0]
        store[(2,) + a] = store[(2,) + a] + via_4[c][0]
        store[6] = store[6] + via_3[c][1]
        store[(6,) + b] = store[(6,) + b] + via_4[c][(1,) + at_b]
        z_later[c] += [
            z_send_to(c, 6, store.at[2], landed[c].at[2], 2),
            z_send_to(c, 7, store.at[6], landed[c].at[3], 6),
        ]

    def summed(c):
        for copy in z_later[c]:
            copy.wait_recv()
        got = landed[c]
        return sums[c][0] + ((got[0] + got[1]) + (got[2] + got[3]))

    def multiply(c):
        part[c] = product(c).reshape(NZ, ROWS, WIDE)
        z_first(c)

    def multiply_last():
        total = product(2)
        part_last[:, 0:ROWS, :] = total[:, 0:128].reshape(NZ, ROWS, 128)
        rest = jnp.concatenate(
            [total[:, 128:144], jnp.zeros((SET, 112), jnp.float32)], axis=1
        )
        for b in range(SET // 128):
            tile = jnp.transpose(rest[128 * b : 128 * b + 128])[0:REST]
            part_last[2 * b, ROWS:PACKED, 0:ROWS] = tile[:, 0:ROWS]
            part_last[2 * b + 1, ROWS:PACKED, 0:ROWS] = tile[:, ROWS : 2 * ROWS]
        z_first(2)

    def code(values, tile, rows):
        most = jnp.maximum(jnp.max(jnp.abs(values), axis=0, keepdims=True), TINY)
        scale[tile : tile + 1, :] = most * (1.0 / TOP)
        codes = jnp.round(values * (TOP / most)).astype(jnp.int32)
        if rows > values.shape[0]:
            codes = jnp.concatenate(
                [codes, jnp.zeros((rows - values.shape[0], 128), jnp.int32)], axis=0
            )
        return codes.astype(jnp.int16)

    turn = grp * (COLS % 128)

    def update(c):
        first = c * WIDE
        total = summed(c)
        driver = drv_in[:, first : first + WIDE].astype(jnp.float32)
        total = (driver + total) / gap[:, first : first + WIDE]
        for j in range(2):
            tile = pltpu.roll(total[:, 128 * j : 128 * j + 128], turn, axis=1)
            lanes = slice(first + 128 * j, first + 128 * j + 128)
            fr[y, :, lanes] = code(tile, 2 * c + j, ROWS)
        cols = pl.ds(first, WIDE)
        y_copies[c] = [
            send(fr.at[y, :, cols], fr.at[y, :, cols], y_send.at[c, d - 1], y_recv.at[c, d - 1], at_y(d))
            for d in FAR
        ]
        cross(fr.at[y, :, cols], out.at[y, core, :, cols], c, 0)

    def cross(src, dst, kind, d):
        c_copies.append(send(src, dst, c_send.at[kind, d], c_recv.at[kind, d], sibling))

    def spread(c):
        cols = pl.ds(c * WIDE, WIDE)
        for copy, d in zip(y_copies[c], FAR):
            copy.wait_recv()
            owner = lax.rem(y + NY - d, NY)
            cross(fr.at[owner, :, cols], out.at[owner, core, :, cols], c, d)
        copy = pltpu.make_async_copy(fr.at[:, :, cols], out.at[:, core, :, cols], o_sem.at[c])
        copy.start()
        o_copies.append(copy)

    def update_last():
        total = (drv_last[...] + summed(2)) / gap_last[...]
        total = jnp.concatenate(
            [pltpu.roll(total[0:ROWS], turn, axis=1), total[ROWS:PACKED]], axis=0
        )
        fr_last[y] = code(total, 4, TILED)
        fr_scale[y] = scale[...]
        copies = []
        for d in FAR:
            for i, ref in enumerate((fr_scale.at[y], fr_last.at[y])):
                copies.append(
                    send(ref, ref, y_send.at[2 + i, d - 1], y_recv.at[2 + i, d - 1], at_y(d))
                )
        cross(fr_scale.at[y], out_scale.at[y, core], 2, 0)
        cross(fr_last.at[y], out_last.at[y, core], 3, 0)
        return copies

    def spread_last(copies):
        for i, d in enumerate(FAR):
            owner = lax.rem(y + NY - d, NY)
            copies[2 * i].wait_recv()
            cross(fr_scale.at[owner], out_scale.at[owner, core], 2, d)
            copies[2 * i + 1].wait_recv()
            cross(fr_last.at[owner], out_last.at[owner, core], 3, d)
        for kind, (src, dst) in enumerate(((fr_scale, out_scale), (fr_last, out_last))):
            copy = pltpu.make_async_copy(src, dst.at[:, core], o_sem.at[2 + kind])
            copy.start()
            o_copies.append(copy)

    scale[...] = jnp.zeros(scale.shape, jnp.float32)
    part_last[:, ROWS:PACKED, :] = jnp.zeros((NZ, REST, 128), jnp.float32)
    multiply(0)
    multiply(1)
    z_direct(0)
    relay(0)
    multiply_last()
    z_direct(1)
    relay(1)
    z_direct(2)
    update(0)
    relay(2)
    update(1)
    last = update_last()
    spread(0)
    spread(1)
    spread_last(last)
    for copy in c_copies:
        copy.wait_recv()
    for copy in o_copies:
        copy.wait()
    for copy in started:
        copy.wait_send()


def place_kernel(codes, last, scale, out):
    tall = out.shape[0]
    rows = pl.ds(pl.multiple_of(pl.program_id(0) * tall, tall), tall)
    lane = lax.broadcasted_iota(jnp.int32, (tall, 128), 1)

    def value(coded):
        return coded.astype(jnp.int32).astype(jnp.float32)

    def tile(g, j):
        at = (g // 2, g % 2)
        coded = codes[at + (slice(None), slice(128 * j, 128 * j + 128))] if j < 4 else last[at + (rows,)]
        return value(coded) * scale[at + (slice(j, j + 1),)]

    rest = [
        value(last[g // 2, g % 2, ROWS:TILED, :])[0:REST] * scale[g // 2, g % 2, 4:5, :]
        for g in range(2 * NY)
    ]
    rest = jnp.transpose(jnp.concatenate(rest, axis=0))
    rest = rest[0:ROWS].reshape(ROWS // tall, tall, 128)
    step = pl.program_id(0)
    mine = rest[0]
    for i in range(1, ROWS // tall):
        mine = jnp.where(step == i, rest[i], mine)

    before = None
    for g in range(2 * NY):
        edge = REST * g
        for j in range(5):
            now = tile(g, j)
            first = 128 * (5 * g + j)
            out[:, first : first + 128] = now if before is None else jnp.where(lane < edge, before, now)
            before = now
        before = jnp.where(lane < edge, before, mine)
    out[:, VP - 128 : VP] = before


def shards(amplitudes, integrals, hole_ints, driver, e_occ, e_virt, occ_pairs, virt_pairs):
    dma = pltpu.SemaphoreType.DMA
    bf16, f32, i16 = jnp.bfloat16, jnp.float32, jnp.int16
    codes, last, scale = pl.pallas_call(
        ladder_kernel,
        out_shape=[
            jax.ShapeDtypeStruct((NY, 2, ROWS, LAST), i16),
            jax.ShapeDtypeStruct((NY, 2, TILED, 128), i16),
            jax.ShapeDtypeStruct((NY, 2, 8, 128), f32),
        ],
        in_specs=[pl.BlockSpec(memory_space=pl.ANY)] * 8,
        out_specs=[pl.BlockSpec(memory_space=pl.ANY)] * 3,
        scratch_shapes=[
            pltpu.VMEM((ROWS, VP), bf16),
            pltpu.VMEM((COLS, DEPTH), bf16),
            pltpu.VMEM((ROWS, COLS), bf16),
            pltpu.VMEM((SET, NX * 128), bf16),
            pltpu.VMEM((1, 128), f32),
            pltpu.VMEM((288,), f32),
            pltpu.VMEM((2, ROWS), jnp.int32),
            pltpu.VMEM((2, COLS), jnp.int32),
            pltpu.VMEM((TALL, LANES), bf16),
            pltpu.VMEM((TALL, DEEP), bf16),
            pltpu.VMEM((NX * 128, FRAME), bf16),
            pltpu.VMEM((NZ, ROWS, DEEP), bf16),
            pltpu.VMEM((NZ, ROWS, DEEP), bf16),
            pltpu.VMEM((SET, NX * 128), bf16),
            pltpu.VMEM((2, NZ, ROWS, WIDE), f32),
            pltpu.VMEM((NZ, PACKED, 128), f32),
            pltpu.VMEM((2, 2, ROWS, WIDE), f32),
            pltpu.VMEM((2, PACKED, 128), f32),
            pltpu.VMEM((2, 2, ROWS, 128), f32),
            pltpu.VMEM((2, 40, 128), f32),
            pltpu.VMEM((2, 4, ROWS, WIDE), f32),
            pltpu.VMEM((4, PACKED, 128), f32),
            pltpu.VMEM((8, 128), f32),
            pltpu.VMEM((NY, ROWS, LAST), i16),
            pltpu.VMEM((NY, TILED, 128), i16),
            pltpu.VMEM((NY, 8, 128), f32),
            pltpu.VMEM((ROWS, COLS), f32),
            pltpu.VMEM((PACKED, 128), f32),
            pltpu.VMEM((PACKED, 128), f32),
            dma((11,)),
            dma((3, 4, 2)), dma((3, 4, 2)),
            dma((7,)), dma((7,)),
            dma((7,)), dma((7,)),
            dma((12,)), dma((12,)),
            dma((3, 8)), dma((3, 8)),
            dma((4, 7)), dma((4, 7)),
            dma((4, 8)), dma((4, 8)),
            dma((4,)),
        ],
        compiler_params=pltpu.CompilerParams(
            collective_id=0, has_side_effects=True, vmem_limit_bytes=62 * 2**20
        ),
        cost_estimate=pl.CostEstimate(
            flops=2 * SET * 4 * (DEPTH + ROWS) * COLS,
            bytes_accessed=8 * 2**20, transcendentals=0,
        ),
    )(
        amplitudes, integrals.T, hole_ints, driver, e_occ.reshape(1, 128),
        e_virt, occ_pairs, virt_pairs,
    )
    tall = 16
    return pl.pallas_call(
        place_kernel,
        grid=(ROWS // tall,),
        out_shape=jax.ShapeDtypeStruct((ROWS, VP), f32),
        in_specs=[
            pl.BlockSpec((NY, 2, tall, LAST), lambda i: (0, 0, i, 0)),
            pl.BlockSpec((NY, 2, TILED, 128), lambda i: (0, 0, 0, 0)),
            pl.BlockSpec((NY, 2, 8, 128), lambda i: (0, 0, 0, 0)),
        ],
        out_specs=pl.BlockSpec((tall, VP), lambda i: (i, 0)),
        compiler_params=pltpu.CompilerParams(vmem_limit_bytes=62 * 2**20),
    )(codes, last, scale)


def solution(mesh):
    placed = (
        P("pair", None),
        P("pair", "grp"),
        P(),
        P("pair", "grp"),
        P(),
        P(),
        P(None, "pair"),
        P(None, "grp"),
    )
    return jax.shard_map(
        shards, mesh=mesh, in_specs=placed, out_specs=P("pair", None), check_vma=False
    )
```

time: 82.1 us -> 73.9 us (0.900)
  Pallas kernels: 80.6 us -> 73.6 us
  local copies, waits for them, and re-layouts: 1.24 us -> 0 us
    pallas_call x1, Pallas kernels: 75.9 us -> 69.7 us  [shards(): pl.pallas_call(ladder_kernel, out_shape=[jax.ShapeDtypeStruct((NY, 2, ROW...]
    reshape x1 -> x0, local copies, waits for them, and re-layouts: 1.24 us -> none  [shards(): e_virt.reshape(1, 288)]
where the time goes in v3:
time: 73.9 us; the launch traced here: 73.7 us
  Pallas kernels  73.6 us (100%)
    pallas_call x1, Pallas kernels, shards(): pl.pallas_call(ladder_kernel, out_shape=[jax.ShapeDtypeStruct((NY, 2, ROW...  69.7 us
    pallas_call x1, Pallas kernels, shards(): pl.pallas_call(place_kernel, grid=(ROWS // tall,), out_shape=jax.ShapeDty...  3.94 us

profile of v3, /device:TPU:1, one launch (start us, length us, event | category | flops | bytes accessed | tf_op | source)
XLA Modules:
  0.0 73.7 jit_solution(1814231363388016471)
XLA Ops:
  0.0 69.7 %shard_map.82 = (s16[8,2,64,512]{3,2,1,0:T(8,128)(2,1)}, s16[8,2,80,128]{3,2,1,0:T(8,128)(2,1)}, f32[8,2,8,128]{3,2,1,0:T(8,128)}) custom-call(bf16[64,10368]{1,0:T(8,128)(2,1)} %amp.1, bf16[648,324]{1,0:T(8,128)(2,1)} %bitcast.2, bf16[2048,2048]{1,0:T(8,128)(2,1)} %holes.1, bf16[64,648]{1,0:T(8,128)(2,1)} %drv.1, f32[1,128]{1,0:T(1,128)} %bitcast.3, ...), custom_call_target="tpu_custom_call" | custom-call | flops 1029832704 | bytes 8388608 | tf_op jit(solution)/shard_map/pallas_call | solution.py:455
  69.7 3.9 %shard_map.83 = f32[64,10368]{1,0:T(8,128)} custom-call(s16[8,2,64,512]{3,2,1,0:T(8,128)(2,1)} %get-tuple-element.8.codes, s16[8,2,80,128]{3,2,1,0:T(8,128)(2,1)} %get-tuple-element.9.last, f32[8,2,8,128]{3,2,1,0:T(8,128)} %get-tuple-element.10.scale), custom_call_target="tpu_custom_call" | custom-call | tf_op jit(solution)/shard_map/pallas_call | solution.py:516

commit v4 on v3

--- a/solution.py
+++ b/solution.py
@@ -225,11 +225,11 @@
     ]
     share(own, 0)
     x_second(0)
-    x_copies[2] = [x_sends(2, x, d, d - 1) for d in (2, 1, 3)]
     for slot, (copy, d) in enumerate(zip(near_copies, (2, 6, 1, 7))):
         copy.wait_recv()
         share(al.at[NZ - d, :, both], 8 + slot)
     x_second(1)
+    x_copies[2] = [x_sends(2, x, d, d - 1) for d in (2, 1, 3)]
     for copy, d in zip(ay_copies, FAR):
         copy.wait_recv()
         rows, lanes = unit_of(lax.rem(y + NY - d, NY))
@@ -413,7 +413,7 @@
         copy.wait_send()
 
 
-def place_kernel(codes, last, scale, out):
+def place_kernel(codes, last, scale, out, rest):
     tall = out.shape[0]
     rows = pl.ds(pl.multiple_of(pl.program_id(0) * tall, tall), tall)
     lane = lax.broadcasted_iota(jnp.int32, (tall, 128), 1)
@@ -426,17 +426,15 @@
         coded = codes[at + (slice(None), slice(128 * j, 128 * j + 128))] if j < 4 else last[at + (rows,)]
         return value(coded) * scale[at + (slice(j, j + 1),)]
 
-    rest = [
-        value(last[g // 2, g % 2, ROWS:TILED, :])[0:REST] * scale[g // 2, g % 2, 4:5, :]
-        for g in range(2 * NY)
-    ]
-    rest = jnp.transpose(jnp.concatenate(rest, axis=0))
-    rest = rest[0:ROWS].reshape(ROWS // tall, tall, 128)
-    step = pl.program_id(0)
-    mine = rest[0]
-    for i in range(1, ROWS // tall):
-        mine = jnp.where(step == i, rest[i], mine)
-
+    @pl.when(pl.program_id(0) == 0)
+    def _():
+        lines = [
+            value(last[g // 2, g % 2, ROWS:TILED, :])[0:REST] * scale[g // 2, g % 2, 4:5, :]
+            for g in range(2 * NY)
+        ]
+        rest[...] = jnp.transpose(jnp.concatenate(lines, axis=0))
+
+    mine = rest[rows, :]
     before = None
     for g in range(2 * NY):
         edge = REST * g
@@ -512,7 +510,7 @@
         amplitudes, integrals.T, hole_ints, driver, e_occ.reshape(1, 128),
         e_virt, occ_pairs, virt_pairs,
     )
-    tall = 16
+    tall = 32
     return pl.pallas_call(
         place_kernel,
         grid=(ROWS // tall,),
@@ -523,6 +521,7 @@
             pl.BlockSpec((NY, 2, 8, 128), lambda i: (0, 0, 0, 0)),
         ],
         out_specs=pl.BlockSpec((tall, VP), lambda i: (i, 0)),
+        scratch_shapes=[pltpu.VMEM((128, 128), f32)],
         compiler_params=pltpu.CompilerParams(vmem_limit_bytes=62 * 2**20),
     )(codes, last, scale)
 

time: 73.9 us -> 69.2 us (0.936)
  Pallas kernels: 73.6 us -> 69 us
    pallas_call x1, Pallas kernels: 69.7 us -> 66.1 us  [shards(): pl.pallas_call(ladder_kernel, out_shape=[jax.ShapeDtypeStruct((NY, 2, ROW...]
    pallas_call x1, Pallas kernels: 3.94 us -> 2.94 us  [shards(): pl.pallas_call(place_kernel, grid=(ROWS // tall,), out_shape=jax.ShapeDty...]
where the time goes in v4:
time: 69.2 us; the launch traced here: 69 us
  Pallas kernels  69 us (100%)
    pallas_call x1, Pallas kernels, shards(): pl.pallas_call(ladder_kernel, out_shape=[jax.ShapeDtypeStruct((NY, 2, ROW...  66.1 us
    pallas_call x1, Pallas kernels, shards(): pl.pallas_call(place_kernel, grid=(ROWS // tall,), out_shape=jax.ShapeDty...  2.94 us

profile of v4, /device:TPU:1, one launch (start us, length us, event | category | flops | bytes accessed | tf_op | source)
XLA Modules:
  0.0 69.0 jit_solution(9719210374121982232)
XLA Ops:
  0.0 66.1 %shard_map.82 = (s16[8,2,64,512]{3,2,1,0:T(8,128)(2,1)}, s16[8,2,80,128]{3,2,1,0:T(8,128)(2,1)}, f32[8,2,8,128]{3,2,1,0:T(8,128)}) custom-call(bf16[64,10368]{1,0:T(8,128)(2,1)} %amp.1, bf16[648,324]{1,0:T(8,128)(2,1)} %bitcast.2, bf16[2048,2048]{1,0:T(8,128)(2,1)} %holes.1, bf16[64,648]{1,0:T(8,128)(2,1)} %drv.1, f32[1,128]{1,0:T(1,128)} %bitcast.3, ...), custom_call_target="tpu_custom_call" | custom-call | flops 1029832704 | bytes 8388608 | tf_op jit(solution)/shard_map/pallas_call | solution.py:453
  66.1 2.9 %shard_map.83 = f32[64,10368]{1,0:T(8,128)} custom-call(s16[8,2,64,512]{3,2,1,0:T(8,128)(2,1)} %get-tuple-element.8.codes, s16[8,2,80,128]{3,2,1,0:T(8,128)(2,1)} %get-tuple-element.9.last, f32[8,2,8,128]{3,2,1,0:T(8,128)} %get-tuple-element.10.scale), custom_call_target="tpu_custom_call" | custom-call | tf_op jit(solution)/shard_map/pallas_call | solution.py:514

commit v5 on v4

--- a/solution.py
+++ b/solution.py
@@ -13,6 +13,7 @@
 COLS = 648
 LANES = 384
 FRAME = 768
+SPARE = LANES - DEPTH
 DEEP = NX * LANES
 TALL = 656
 VP = 10368
@@ -28,7 +29,7 @@
 
 def ladder_kernel(
     amp, ints, holes, drv, eocc, evirt, opairs, vpairs, out, out_last, out_scale,
-    amp_in, ints_in, drv_in, hole_win, eocc_in, evirt_in, opairs_in, vpairs_in,
+    amp_in, ints_in, drv_in, hole_own, hole_win, eocc_in, evirt_in, opairs_in, vpairs_in,
     own_vt, vt, ra, ap, al, hole_rel, part, part_last, via3, via3_last, via4, via4_last, rs, rs_last,
     scale, fr, fr_last, fr_scale, gap, gap_last, drv_last,
     in_sem, x_send, x_recv, a_send, a_recv, ay_send, ay_recv, ad_send, ad_recv,
@@ -58,7 +59,10 @@
     loads = [
         pltpu.make_async_copy(ints, ints_in, in_sem.at[0]),
         pltpu.make_async_copy(amp, amp_in, in_sem.at[1]),
-        pltpu.make_async_copy(drv, drv_in, in_sem.at[2]),
+        pltpu.make_async_copy(
+            holes.at[pl.ds(pl.multiple_of(pair * ROWS, ROWS), ROWS)], hole_own, in_sem.at[2]
+        ),
+        pltpu.make_async_copy(drv, drv_in, in_sem.at[11]),
         pltpu.make_async_copy(eocc, eocc_in, in_sem.at[3]),
         pltpu.make_async_copy(evirt, evirt_in, in_sem.at[4]),
         pltpu.make_async_copy(opairs, opairs_in, in_sem.at[5]),
@@ -75,8 +79,7 @@
     for load in loads:
         load.start()
 
-    half = pl.multiple_of(lax.rem(z, 2) * ROWS, ROWS)
-    other = pl.multiple_of(ROWS - lax.rem(z, 2) * ROWS, ROWS)
+    half = lax.rem(z, 2) * ROWS + ROWS - 16
     started = []
 
     def send(src, dst, send_sem, recv_sem, device):
@@ -97,16 +100,35 @@
     start = pl.multiple_of(grp * (COLS // 128) * 128, 128)
     window = amp_in[:, pl.ds(start, FRAME)].astype(jnp.float32)
     window = pltpu.roll(window, lax.rem(FRAME - grp * (COLS % 128), FRAME), axis=1)
+    row = lax.broadcasted_iota(jnp.int32, (16, FRAME), 0)
+    tail = jnp.where(row < SPARE - (ROWS - 16), 0.0, window[ROWS - 16 : ROWS])
+    other = ROWS * (1 - lax.rem(z, 2)) + ROWS - 16
     for k in range(NX):
-        ra[pl.ds(128 * k + other, ROWS), :] = jnp.zeros((ROWS, FRAME), jnp.bfloat16)
-    ra[pl.ds(128 * x + half, ROWS), :] = window.astype(jnp.bfloat16)
-
+        for b in range(2):
+            at = 128 * k + ROWS * b
+            ra[at : at + ROWS - 16, :] = jnp.zeros((ROWS - 16, FRAME), jnp.bfloat16)
+        ra[pl.ds(pl.multiple_of(128 * k + other, 16), 16), :] = jnp.zeros((16, FRAME), jnp.bfloat16)
+    ra[pl.ds(pl.multiple_of(128 * x + half, 16), 16), :] = tail.astype(jnp.bfloat16)
+    lane = lax.broadcasted_iota(jnp.int32, (128, 128), 1)
+    for b in range(FRAME // 128):
+        tall = min(128, TALL - 128 * b)
+        block = jnp.concatenate(
+            [window[:, 128 * b : 128 * b + 128], jnp.zeros((128 - ROWS, 128), jnp.float32)], axis=0
+        )
+        block = pltpu.roll(jnp.transpose(block), DEPTH - 256, axis=1)[0:tall]
+        lines = slice(128 * b, 128 * b + tall)
+        mixed = jnp.where(
+            lane[0:tall] < DEPTH - 256, own_vt[lines, 256:LANES].astype(jnp.float32), block
+        )
+        own_vt[lines, 256:LANES] = mixed.astype(jnp.bfloat16)
+
+    loads[2].wait()
     for k in range(NX):
         for t in range(NZ):
-            first = (k * NZ + t) * DEPTH
+            owner = k * NZ + t
             at = k * LANES
-            ap[t, :, at + 256 : at + LANES] = jnp.zeros((ROWS, LANES - 256), jnp.bfloat16)
-            ap[t, :, at : at + DEPTH] = amp_in[:, first : first + DEPTH]
+            ap[t, :, at : at + DEPTH] = amp_in[:, owner * DEPTH : (owner + 1) * DEPTH]
+            ap[t, :, at + DEPTH : at + LANES] = hole_own[:, owner * ROWS : owner * ROWS + SPARE]
 
     pl.semaphore_wait(barrier, len(peers))
 
@@ -128,7 +150,7 @@
         if side is not None:
             first, tall, wide = first + 128 * side, 128, 128
         to = vt.at[pl.ds(first, tall), pl.ds(pl.multiple_of(owner * LANES, 128), LANES)]
-        cells = ra.at[pl.ds(pl.multiple_of(128 * owner + half, ROWS), ROWS), pl.ds(first, wide)]
+        cells = ra.at[pl.ds(pl.multiple_of(128 * owner + half, 16), 16), pl.ds(first, wide)]
         return [
             send(own_vt.at[pl.ds(first, tall)] if owner is x else to, to,
                  x_send.at[c, slot, 0], x_recv.at[c, slot, 0], at_x(d)),
@@ -160,7 +182,7 @@
     vt[:, pl.ds(pl.multiple_of(x * LANES, 128), LANES)] = own_vt[...]
     al[0] = ap[z]
 
-    for load in loads[2:]:
+    for load in loads[3:]:
         load.wait()
     orbital = lax.broadcasted_iota(jnp.int32, (128, 128), 0)
     diagonal = orbital == lax.broadcasted_iota(jnp.int32, (128, 128), 1)
@@ -330,6 +352,23 @@
 
     turn = grp * (COLS % 128)
 
+    def y_move(c, i, owner, cols, d):
+        ref = fr.at[owner, :, cols]
+        return send(ref, ref, y_send.at[c, i], y_recv.at[c, i], at_y(d))
+
+    def back(d):
+        return lax.rem(y + NY - d, NY)
+
+    def y_relay(c):
+        first = c * WIDE
+        cols, left, right = pl.ds(first, WIDE), pl.ds(first, 128), pl.ds(first + 128, 128)
+        later = []
+        for i, (d, side, on) in enumerate(((2, left, 1), (6, right, 7))):
+            y_copies[c][i].wait_recv()
+            later.append(y_move(c, 4 + i, back(d), side, d))
+            later.append(y_move(c, 6 + i, back(d), cols, on))
+        y_copies[c] += later
+
     def update(c):
         first = c * WIDE
         total = summed(c)
@@ -340,10 +379,7 @@
             lanes = slice(first + 128 * j, first + 128 * j + 128)
             fr[y, :, lanes] = code(tile, 2 * c + j, ROWS)
         cols = pl.ds(first, WIDE)
-        y_copies[c] = [
-            send(fr.at[y, :, cols], fr.at[y, :, cols], y_send.at[c, d - 1], y_recv.at[c, d - 1], at_y(d))
-            for d in FAR
-        ]
+        y_copies[c] = [y_move(c, i, y, cols, d) for i, d in enumerate((2, 6, 1, 7))]
         cross(fr.at[y, :, cols], out.at[y, core, :, cols], c, 0)
 
     def cross(src, dst, kind, d):
@@ -351,10 +387,11 @@
 
     def spread(c):
         cols = pl.ds(c * WIDE, WIDE)
-        for copy, d in zip(y_copies[c], FAR):
-            copy.wait_recv()
-            owner = lax.rem(y + NY - d, NY)
-            cross(fr.at[owner, :, cols], out.at[owner, core, :, cols], c, d)
+        copies = y_copies[c]
+        for waits, d in (((), 2), ((), 6), ((2,), 1), ((3,), 7), ((5,), 3), ((7,), 5), ((4, 6), 4)):
+            for i in waits:
+                copies[i].wait_recv()
+            cross(fr.at[back(d), :, cols], out.at[back(d), core, :, cols], c, d)
         copy = pltpu.make_async_copy(fr.at[:, :, cols], out.at[:, core, :, cols], o_sem.at[c])
         copy.start()
         o_copies.append(copy)
@@ -401,7 +438,9 @@
     update(0)
     relay(2)
     update(1)
+    y_relay(0)
     last = update_last()
+    y_relay(1)
     spread(0)
     spread(1)
     spread_last(last)
@@ -463,6 +502,7 @@
             pltpu.VMEM((ROWS, VP), bf16),
             pltpu.VMEM((COLS, DEPTH), bf16),
             pltpu.VMEM((ROWS, COLS), bf16),
+            pltpu.VMEM((ROWS, SET * NX), bf16),
             pltpu.VMEM((SET, NX * 128), bf16),
             pltpu.VMEM((1, 128), f32),
             pltpu.VMEM((288,), f32),
@@ -489,13 +529,13 @@
             pltpu.VMEM((ROWS, COLS), f32),
             pltpu.VMEM((PACKED, 128), f32),
             pltpu.VMEM((PACKED, 128), f32),
-            dma((11,)),
+            dma((12,)),
             dma((3, 4, 2)), dma((3, 4, 2)),
             dma((7,)), dma((7,)),
             dma((7,)), dma((7,)),
             dma((12,)), dma((12,)),
             dma((3, 8)), dma((3, 8)),
-            dma((4, 7)), dma((4, 7)),
+            dma((4, 8)), dma((4, 8)),
             dma((4, 8)), dma((4, 8)),
             dma((4,)),
         ],

time: 69.2 us -> 65.3 us (0.944)
  Pallas kernels: 69 us -> 65.1 us
    pallas_call x1, Pallas kernels: 66.1 us -> 62.2 us  [shards(): pl.pallas_call(ladder_kernel, out_shape=[jax.ShapeDtypeStruct((NY, 2, ROW...]
where the time goes in v5:
time: 65.3 us; the launch traced here: 65.1 us
  Pallas kernels  65.1 us (100%)
    pallas_call x1, Pallas kernels, shards(): pl.pallas_call(ladder_kernel, out_shape=[jax.ShapeDtypeStruct((NY, 2, ROW...  62.2 us
    pallas_call x1, Pallas kernels, shards(): pl.pallas_call(place_kernel, grid=(ROWS // tall,), out_shape=jax.ShapeDty...  2.94 us

profile of v5, /device:TPU:1, one launch (start us, length us, event | category | flops | bytes accessed | tf_op | source)
XLA Modules:
  0.0 65.1 jit_solution(6338033496687992904)
XLA Ops:
  0.0 62.2 %shard_map.82 = (s16[8,2,64,512]{3,2,1,0:T(8,128)(2,1)}, s16[8,2,80,128]{3,2,1,0:T(8,128)(2,1)}, f32[8,2,8,128]{3,2,1,0:T(8,128)}) custom-call(bf16[64,10368]{1,0:T(8,128)(2,1)} %amp.1, bf16[648,324]{1,0:T(8,128)(2,1)} %bitcast.2, bf16[2048,2048]{1,0:T(8,128)(2,1)} %holes.1, bf16[64,648]{1,0:T(8,128)(2,1)} %drv.1, f32[1,128]{1,0:T(1,128)} %bitcast.3, ...), custom_call_target="tpu_custom_call" | custom-call | flops 1029832704 | bytes 8388608 | tf_op jit(solution)/shard_map/pallas_call | solution.py:492
  62.2 2.9 %shard_map.83 = f32[64,10368]{1,0:T(8,128)} custom-call(s16[8,2,64,512]{3,2,1,0:T(8,128)(2,1)} %get-tuple-element.8.codes, s16[8,2,80,128]{3,2,1,0:T(8,128)(2,1)} %get-tuple-element.9.last, f32[8,2,8,128]{3,2,1,0:T(8,128)} %get-tuple-element.10.scale), custom_call_target="tpu_custom_call" | custom-call | tf_op jit(solution)/shard_map/pallas_call | solution.py:554

commit v6 on v5

--- a/solution.py
+++ b/solution.py
@@ -25,13 +25,14 @@
 TOP = 32767.0
 TINY = 1e-33
 FAR = (4, 3, 5, 2, 6, 1, 7)
+NEAR = FAR[::-1]
 
 
 def ladder_kernel(
-    amp, ints, holes, drv, eocc, evirt, opairs, vpairs, out, out_last, out_scale,
+    amp, ints, holes, drv, eocc, evirt, opairs, vpairs, out, out_last,
     amp_in, ints_in, drv_in, hole_own, hole_win, eocc_in, evirt_in, opairs_in, vpairs_in,
     own_vt, vt, ra, ap, al, hole_rel, part, part_last, via3, via3_last, via4, via4_last, rs, rs_last,
-    scale, fr, fr_last, fr_scale, gap, gap_last, drv_last,
+    scale, fr, fr_last, gap, gap_last, drv_last,
     in_sem, x_send, x_recv, a_send, a_recv, ay_send, ay_recv, ad_send, ad_recv,
     z_send, z_recv, y_send, y_recv, c_send, c_recv, o_sem,
 ):
@@ -49,12 +50,6 @@
         return (lax.rem(y + d, NY) * 2 + core, pair)
 
     sibling = (y * 2 + 1 - core, pair)
-
-    barrier = pltpu.get_barrier_semaphore()
-    peers = [at_x(d) for d in (1, 2, 3)] + [at_z(d) for d in FAR]
-    peers += [at_y(d) for d in FAR] + [sibling]
-    for peer in peers:
-        pl.semaphore_signal(barrier, inc=1, device_id=peer, device_id_type=MESH)
 
     loads = [
         pltpu.make_async_copy(ints, ints_in, in_sem.at[0]),
@@ -76,11 +71,24 @@
                 holes.at[rows, cols], hole_win.at[:, pl.ds(128 * k, 128)], in_sem.at[7 + k]
             )
         )
-    for load in loads:
+    for load in loads[:3]:
+        load.start()
+
+    barrier = pltpu.get_barrier_semaphore()
+    peers = [at_x(d) for d in (1, 2, 3)] + [at_z(d) for d in FAR]
+    peers += [at_y(d) for d in FAR] + [sibling]
+    for peer in peers:
+        pl.semaphore_signal(barrier, inc=1, device_id=peer, device_id_type=MESH)
+    for load in loads[3:]:
         load.start()
 
     half = lax.rem(z, 2) * ROWS + ROWS - 16
     started = []
+
+    def settle(count):
+        for copy in started[:count]:
+            copy.wait_send()
+        del started[:count]
 
     def send(src, dst, send_sem, recv_sem, device):
         copy = pltpu.make_async_remote_copy(
@@ -247,13 +255,14 @@
     ]
     share(own, 0)
     x_second(0)
-    for slot, (copy, d) in enumerate(zip(near_copies, (2, 6, 1, 7))):
-        copy.wait_recv()
+    for slot, d in ((2, 1), (3, 7), (0, 2), (1, 6)):
+        near_copies[slot].wait_recv()
         share(al.at[NZ - d, :, both], 8 + slot)
     x_second(1)
+    before = len(started)
     x_copies[2] = [x_sends(2, x, d, d - 1) for d in (2, 1, 3)]
-    for copy, d in zip(ay_copies, FAR):
-        copy.wait_recv()
+    for d in NEAR:
+        ay_copies[FAR.index(d)].wait_recv()
         rows, lanes = unit_of(lax.rem(y + NY - d, NY))
         share(al.at[far, rows, lanes], d)
     for copy in ad_copies:
@@ -340,15 +349,11 @@
             part_last[2 * b + 1, ROWS:PACKED, 0:ROWS] = tile[:, ROWS : 2 * ROWS]
         z_first(2)
 
-    def code(values, tile, rows):
+    def code(values, tile):
         most = jnp.maximum(jnp.max(jnp.abs(values), axis=0, keepdims=True), TINY)
-        scale[tile : tile + 1, :] = most * (1.0 / TOP)
-        codes = jnp.round(values * (TOP / most)).astype(jnp.int32)
-        if rows > values.shape[0]:
-            codes = jnp.concatenate(
-                [codes, jnp.zeros((rows - values.shape[0], 128), jnp.int32)], axis=0
-            )
-        return codes.astype(jnp.int16)
+        power = jnp.ceil(jnp.log2(most) + 1e-3)
+        scale[tile : tile + 1, :] = power
+        return jnp.round(values * (TOP * jnp.exp2(-power))).astype(jnp.int32)
 
     turn = grp * (COLS % 128)
 
@@ -377,7 +382,7 @@
         for j in range(2):
             tile = pltpu.roll(total[:, 128 * j : 128 * j + 128], turn, axis=1)
             lanes = slice(first + 128 * j, first + 128 * j + 128)
-            fr[y, :, lanes] = code(tile, 2 * c + j, ROWS)
+            fr[y, :, lanes] = code(tile, 2 * c + j).astype(jnp.int16)
         cols = pl.ds(first, WIDE)
         y_copies[c] = [y_move(c, i, y, cols, d) for i, d in enumerate((2, 6, 1, 7))]
         cross(fr.at[y, :, cols], out.at[y, core, :, cols], c, 0)
@@ -401,35 +406,30 @@
         total = jnp.concatenate(
             [pltpu.roll(total[0:ROWS], turn, axis=1), total[ROWS:PACKED]], axis=0
         )
-        fr_last[y] = code(total, 4, TILED)
-        fr_scale[y] = scale[...]
-        copies = []
-        for d in FAR:
-            for i, ref in enumerate((fr_scale.at[y], fr_last.at[y])):
-                copies.append(
-                    send(ref, ref, y_send.at[2 + i, d - 1], y_recv.at[2 + i, d - 1], at_y(d))
-                )
-        cross(fr_scale.at[y], out_scale.at[y, core], 2, 0)
-        cross(fr_last.at[y], out_last.at[y, core], 3, 0)
+        codes = code(total, 4)
+        powers = scale[...].astype(jnp.int32)
+        fr_last[y] = jnp.concatenate([codes, powers], axis=0).astype(jnp.int16)
+        ref = fr_last.at[y]
+        copies = [
+            send(ref, ref, y_send.at[2, d - 1], y_recv.at[2, d - 1], at_y(d)) for d in FAR
+        ]
+        cross(ref, out_last.at[y, core], 2, 0)
         return copies
 
     def spread_last(copies):
-        for i, d in enumerate(FAR):
-            owner = lax.rem(y + NY - d, NY)
-            copies[2 * i].wait_recv()
-            cross(fr_scale.at[owner], out_scale.at[owner, core], 2, d)
-            copies[2 * i + 1].wait_recv()
-            cross(fr_last.at[owner], out_last.at[owner, core], 3, d)
-        for kind, (src, dst) in enumerate(((fr_scale, out_scale), (fr_last, out_last))):
-            copy = pltpu.make_async_copy(src, dst.at[:, core], o_sem.at[2 + kind])
-            copy.start()
-            o_copies.append(copy)
+        for d in NEAR:
+            copies[FAR.index(d)].wait_recv()
+            cross(fr_last.at[back(d)], out_last.at[back(d), core], 2, d)
+        copy = pltpu.make_async_copy(fr_last, out_last.at[:, core], o_sem.at[2])
+        copy.start()
+        o_copies.append(copy)
 
     scale[...] = jnp.zeros(scale.shape, jnp.float32)
     part_last[:, ROWS:PACKED, :] = jnp.zeros((NZ, REST, 128), jnp.float32)
     multiply(0)
     multiply(1)
     z_direct(0)
+    settle(before)
     relay(0)
     multiply_last()
     z_direct(1)
@@ -437,9 +437,11 @@
     z_direct(2)
     update(0)
     relay(2)
+    before = len(started)
     update(1)
     y_relay(0)
     last = update_last()
+    settle(before)
     y_relay(1)
     spread(0)
     spread(1)
@@ -452,7 +454,7 @@
         copy.wait_send()
 
 
-def place_kernel(codes, last, scale, out, rest):
+def place_kernel(codes, last, out, rest):
     tall = out.shape[0]
     rows = pl.ds(pl.multiple_of(pl.program_id(0) * tall, tall), tall)
     lane = lax.broadcasted_iota(jnp.int32, (tall, 128), 1)
@@ -460,17 +462,17 @@
     def value(coded):
         return coded.astype(jnp.int32).astype(jnp.float32)
 
+    ends = [value(last[g // 2, g % 2, ROWS:TILED, :]) for g in range(2 * NY)]
+    scale = [jnp.exp2(end[REST : 2 * REST]) * (1.0 / TOP) for end in ends]
+
     def tile(g, j):
         at = (g // 2, g % 2)
         coded = codes[at + (slice(None), slice(128 * j, 128 * j + 128))] if j < 4 else last[at + (rows,)]
-        return value(coded) * scale[at + (slice(j, j + 1),)]
+        return value(coded) * scale[g][j : j + 1]
 
     @pl.when(pl.program_id(0) == 0)
     def _():
-        lines = [
-            value(last[g // 2, g % 2, ROWS:TILED, :])[0:REST] * scale[g // 2, g % 2, 4:5, :]
-            for g in range(2 * NY)
-        ]
+        lines = [ends[g][0:REST] * scale[g][4:5] for g in range(2 * NY)]
         rest[...] = jnp.transpose(jnp.concatenate(lines, axis=0))
 
     mine = rest[rows, :]
@@ -489,15 +491,14 @@
 def shards(amplitudes, integrals, hole_ints, driver, e_occ, e_virt, occ_pairs, virt_pairs):
     dma = pltpu.SemaphoreType.DMA
     bf16, f32, i16 = jnp.bfloat16, jnp.float32, jnp.int16
-    codes, last, scale = pl.pallas_call(
+    codes, last = pl.pallas_call(
         ladder_kernel,
         out_shape=[
             jax.ShapeDtypeStruct((NY, 2, ROWS, LAST), i16),
             jax.ShapeDtypeStruct((NY, 2, TILED, 128), i16),
-            jax.ShapeDtypeStruct((NY, 2, 8, 128), f32),
         ],
         in_specs=[pl.BlockSpec(memory_space=pl.ANY)] * 8,
-        out_specs=[pl.BlockSpec(memory_space=pl.ANY)] * 3,
+        out_specs=[pl.BlockSpec(memory_space=pl.ANY)] * 2,
         scratch_shapes=[
             pltpu.VMEM((ROWS, VP), bf16),
             pltpu.VMEM((COLS, DEPTH), bf16),
@@ -525,7 +526,6 @@
             pltpu.VMEM((8, 128), f32),
             pltpu.VMEM((NY, ROWS, LAST), i16),
             pltpu.VMEM((NY, TILED, 128), i16),
-            pltpu.VMEM((NY, 8, 128), f32),
             pltpu.VMEM((ROWS, COLS), f32),
             pltpu.VMEM((PACKED, 128), f32),
             pltpu.VMEM((PACKED, 128), f32),
@@ -535,9 +535,9 @@
             dma((7,)), dma((7,)),
             dma((12,)), dma((12,)),
             dma((3, 8)), dma((3, 8)),
-            dma((4, 8)), dma((4, 8)),
-            dma((4, 8)), dma((4, 8)),
-            dma((4,)),
+            dma((3, 8)), dma((3, 8)),
+            dma((3, 8)), dma((3, 8)),
+            dma((3,)),
         ],
         compiler_params=pltpu.CompilerParams(
             collective_id=0, has_side_effects=True, vmem_limit_bytes=62 * 2**20
@@ -558,12 +558,11 @@
         in_specs=[
             pl.BlockSpec((NY, 2, tall, LAST), lambda i: (0, 0, i, 0)),
             pl.BlockSpec((NY, 2, TILED, 128), lambda i: (0, 0, 0, 0)),
-            pl.BlockSpec((NY, 2, 8, 128), lambda i: (0, 0, 0, 0)),
         ],
         out_specs=pl.BlockSpec((tall, VP), lambda i: (i, 0)),
         scratch_shapes=[pltpu.VMEM((128, 128), f32)],
         compiler_params=pltpu.CompilerParams(vmem_limit_bytes=62 * 2**20),
-    )(codes, last, scale)
+    )(codes, last)
 
 
 def solution(mesh):

time: 65.3 us -> 64.3 us (0.985)
  Pallas kernels: 65.1 us -> 64.2 us
    pallas_call x1, Pallas kernels: 62.2 us -> 61.2 us  [shards(): pl.pallas_call(ladder_kernel, out_shape=[jax.ShapeDtypeStruct((NY, 2, ROW...]
where the time goes in v6:
time: 64.3 us; the launch traced here: 64.2 us
  Pallas kernels  64.2 us (100%)
    pallas_call x1, Pallas kernels, shards(): pl.pallas_call(ladder_kernel, out_shape=[jax.ShapeDtypeStruct((NY, 2, ROW...  61.2 us
    pallas_call x1, Pallas kernels, shards(): pl.pallas_call(place_kernel, grid=(ROWS // tall,), out_shape=jax.ShapeDty...  2.95 us

profile of v6, /device:TPU:1, one launch (start us, length us, event | category | flops | bytes accessed | tf_op | source)
XLA Modules:
  0.0 64.2 jit_solution(523656839594582058)
XLA Ops:
  0.0 61.2 %shard_map.82 = (s16[8,2,64,512]{3,2,1,0:T(8,128)(2,1)}, s16[8,2,80,128]{3,2,1,0:T(8,128)(2,1)}) custom-call(bf16[64,10368]{1,0:T(8,128)(2,1)} %amp.1, bf16[648,324]{1,0:T(8,128)(2,1)} %bitcast.2, bf16[2048,2048]{1,0:T(8,128)(2,1)} %holes.1, bf16[64,648]{1,0:T(8,128)(2,1)} %drv.1, f32[1,128]{1,0:T(1,128)} %bitcast.3, f32[288]{0:T(512)} %evirt.1, ...), custom_call_target="tpu_custom_call" | custom-call | flops 1029832704 | bytes 8388608 | tf_op jit(solution)/shard_map/pallas_call | solution.py:494
  61.2 3.0 %shard_map.83 = f32[64,10368]{1,0:T(8,128)} custom-call(s16[8,2,64,512]{3,2,1,0:T(8,128)(2,1)} %get-tuple-element.7.codes, s16[8,2,80,128]{3,2,1,0:T(8,128)(2,1)} %get-tuple-element.8.last), custom_call_target="tpu_custom_call" | custom-call | tf_op jit(solution)/shard_map/pallas_call | solution.py:554
